TPU v7x, 32 devices: a whole 2x2x4 slice. The times are simulated.
32 devices in a mesh: gx: 8 (over z, y), gy: 2 (over x), gz: 2 (over core).
Axes of the slice: x: 2, y: 2, z: 4, core: 2. Of those that a mesh axis runs over, the one named last changes fastest.
Arguments:
- tokens: bfloat16 [64, 32, 128, 128], P('gx', 'gy', 'gz'), may hold values from -6 to 6
- w_qkv: bfloat16 [128, 384], replicated, may hold values from -0.5 to 0.5
- w_out: bfloat16 [128, 128], replicated, may hold values from -0.5 to 0.5
- w_gate_up: bfloat16 [128, 1024], replicated, may hold values from -0.5 to 0.5
- w_down: bfloat16 [512, 128], replicated, may hold values from -0.25 to 0.25
Outputs:
- updated: bfloat16 [64, 32, 128, 128], P('gx', 'gy', 'gz')
All inputs are finite; a program needn't handle non-finite values.
Results may differ from a plain program's by a relative error of at most 0.014.
Values may be sent and summed in bfloat16 or wider, within the bound.
A program may use at most 64 MiB of HBM per device.

v0:
```python
import math

import jax
import jax.numpy as jnp
from jax import lax
from jax.sharding import PartitionSpec as P

HEADS = 8
FF = 512


EPS = 1e-05


def norm_rows(values):
    mean = jnp.mean(values, axis=-1, keepdims=True)
    centred = values - mean
    spread = jnp.mean(centred * centred, axis=-1, keepdims=True)
    return centred * lax.rsqrt(spread + EPS)


def unit_scale(values):
    return values * lax.rsqrt(jnp.mean(values * values) + 1e-06)


def make_kernel(pooled, length):
    width = pooled.shape[1] // 2
    head_dim = width // HEADS
    query = unit_scale(pooled[:, :width]).reshape(length, HEADS, head_dim)
    key_part = unit_scale(pooled[:, width:]).reshape(length, HEADS, head_dim)
    kernel = jnp.einsum("ahd,bhd->hab", query, key_part, precision=lax.Precision.HIGHEST)
    return (kernel / math.sqrt(head_dim * length)).astype(jnp.bfloat16)


def apply_first(kernel, block):
    split = block.reshape(block.shape[0], -1, HEADS, block.shape[-1] // HEADS)
    mixed = jnp.einsum("hab,bmhd->amhd", kernel, split, preferred_element_type=jnp.float32)
    return mixed.reshape((kernel.shape[1],) + block.shape[1:])


def apply_middle(kernel, block):
    split = block.reshape(block.shape[0], block.shape[1], -1, HEADS, block.shape[-1] // HEADS)
    mixed = jnp.einsum("hab,xbmhd->xamhd", kernel, split, preferred_element_type=jnp.float32)
    return mixed.reshape((block.shape[0], kernel.shape[1]) + block.shape[2:])


def apply_third(kernel, block):
    split = block.reshape(
        block.shape[0], block.shape[1], block.shape[2], HEADS, block.shape[-1] // HEADS
    )
    mixed = jnp.einsum("hab,xybhd->xyahd", kernel, split, preferred_element_type=jnp.float32)
    return mixed.reshape(block.shape[0], block.shape[1], kernel.shape[1], block.shape[-1])


def finish(mixed, slab, w_out, w_gate_up, w_down):
    width = slab.shape[-1]
    resid = slab.astype(jnp.float32).reshape(-1, width) + jnp.dot(
        mixed.reshape(-1, width), w_out, preferred_element_type=jnp.float32
    )
    inner = norm_rows(resid).astype(jnp.bfloat16)
    both = jnp.dot(inner, w_gate_up, preferred_element_type=jnp.float32)
    hidden = (jax.nn.gelu(both[:, :FF]) * both[:, FF:]).astype(jnp.bfloat16)
    result = resid + jnp.dot(hidden, w_down, preferred_element_type=jnp.float32)
    return result.astype(jnp.bfloat16).reshape(slab.shape)


def body(tokens, w_qkv, w_out, w_gate_up, w_down):
    rows_x, rows_y, rows_z, width = tokens.shape
    count_x = lax.axis_size("gx")
    count_y = lax.axis_size("gy")
    line_x = rows_x * count_x
    line_y = rows_y * count_y
    line_z = rows_z * lax.axis_size("gz")

    def project(slab):
        normed = norm_rows(slab.astype(jnp.float32)).astype(jnp.bfloat16)
        qkv = jnp.dot(normed.reshape(-1, width), w_qkv, preferred_element_type=jnp.float32)
        qkv = qkv.reshape(rows_y, rows_z, 3 * width)
        both = qkv[..., : 2 * width]
        return (
            qkv[..., 2 * width :].astype(jnp.bfloat16),
            jnp.sum(both, axis=(0, 1)),
            jnp.sum(both, axis=1),
            jnp.sum(both, axis=0),
        )

    value, part_x, part_y, part_z = lax.map(project, tokens)
    part_y = jnp.sum(part_y, axis=0)
    part_z = jnp.sum(part_z, axis=0)
    total_x = lax.psum(part_x, ("gy", "gz"))
    total_y = lax.psum(part_y, ("gx", "gz"))
    total_z = lax.psum(part_z, ("gx", "gy"))
    pooled_x = lax.all_gather(total_x, "gx", axis=0, tiled=True)
    pooled_y = lax.all_gather(total_y, "gy", axis=0, tiled=True)
    pooled_z = lax.all_gather(total_z.astype(jnp.bfloat16), "gz", axis=0, tiled=True).astype(
        total_z.dtype
    )
    kernel_x = make_kernel(pooled_x, line_x)
    kernel_y = make_kernel(pooled_y, line_y)
    kernel_z = make_kernel(pooled_z, line_z)
    x_mixed = apply_first(
        kernel_x, lax.all_to_all(value, "gx", split_axis=1, concat_axis=0, tiled=True)
    ).astype(jnp.bfloat16)
    y_whole = lax.all_to_all(x_mixed, ("gx", "gy"), split_axis=0, concat_axis=1, tiled=True)
    heads = kernel_y.shape[0]
    reordered = kernel_y.reshape(heads, line_y, count_y, count_x, rows_y // count_x)
    reordered = jnp.transpose(reordered, (0, 1, 3, 2, 4)).reshape(heads, line_y, line_y)
    y_mixed = apply_middle(reordered, y_whole).astype(jnp.bfloat16)
    after_y = lax.all_to_all(y_mixed, "gy", split_axis=1, concat_axis=0, tiled=True)
    applied = apply_third(
        kernel_z, lax.all_to_all(after_y, "gz", split_axis=0, concat_axis=2, tiled=True)
    ).astype(jnp.bfloat16)
    mixed = lax.all_to_all(applied, "gz", split_axis=2, concat_axis=0, tiled=True)

    def closing(pair):
        block, slab = pair
        return finish(block, slab, w_out, w_gate_up, w_down)

    return lax.map(closing, (mixed, tokens))


def solution(mesh):
    in_specs = (P("gx", "gy", "gz", None), P(), P(), P(), P())
    out_specs = P("gx", "gy", "gz", None)
    return jax.shard_map(body, mesh=mesh, in_specs=in_specs, out_specs=out_specs, check_vma=False)
```

profile of v0, /device:TPU:0, one launch (start us, length us, event | category | flops | bytes accessed | tf_op | source)
XLA Modules:
  0.0 426.9 jit_solution(9375494609182543575)
XLA Ops:
  0.0 40.3 %while.26 = (s32[]{:T(128)}, bf16[8,16,64,128]{3,2,0,1:T(8,128)(2,1)}, f32[8,256]{1,0:T(8,128)S(1)}, f32[8,16,256]{2,1,0:T(8,128)S(1)}, f32[8,64,256]{2,1,0:T(8,...) while((s32[]{:T(128)}, ...), condition=%wide.region_6.7_spmd, body=%wide.region_0.6_spmd.sunk | while | flops 102740736 | bytes 4317297 | solution.py:87
  1.2 1.3 fusion.79
  2.5 1.5 fusion.80
  5.0 1.2 convert_reduce_fusion.2
  6.2 1.3 fusion.79
  7.6 1.5 fusion.80
  10.1 1.2 convert_reduce_fusion.2
  11.3 1.3 fusion.79
  12.6 1.5 fusion.80
  15.1 1.2 convert_reduce_fusion.2
  16.3 1.3 fusion.79
  17.7 1.5 fusion.80
  20.2 1.2 convert_reduce_fusion.2
  21.4 1.3 fusion.79
  22.7 1.5 fusion.80
  25.2 1.2 convert_reduce_fusion.2
  26.4 1.3 fusion.79
  27.8 1.5 fusion.80
  30.3 1.2 convert_reduce_fusion.2
  31.4 1.3 fusion.79
  32.8 1.5 fusion.80
  36.5 1.3 fusion.79
  37.8 1.5 fusion.80
  40.4 7.3 %all-to-all-start = ((bf16[8,16,64,128]{3,2,0,1:T(8,128)(2,1)}), bf16[8,16,64,128]{3,2,0,1:T(8,128)(2,1)S(1)}, u32[]{:S(2)}, u32[]{:S(2)}) async-start(bf16[8,16,64,128]{3,2,0,1:T(8,128)(2,1)} %get-tuple-element.82), calls=%async_computation | async-start | bytes 4194304 | tf_op jit(solution)/shard_map/all_to_all | solution.py:102
  47.6 6.7 %psum.21 = f32[8,256]{1,0:T(8,128)S(1)} all-reduce(f32[8,256]{1,0:T(8,128)S(1)} %get-tuple-element.83), channel_id=1, replica_groups=mesh['gx'=8,'gy'=2,'gz'=2] {'gy','gz'}, use_global_device_ids=true, to_apply=%region_7.8 | all-reduce | flops 2048 | bytes 16384 | tf_op jit(solution)/shard_map/psum | solution.py:90
  54.3 61.6 %all_gather.9 = f32[64,256]{1,0:T(8,128)S(1)} all-gather(f32[8,256]{1,0:T(8,128)S(1)} %psum.21), channel_id=1, replica_groups=mesh['gx'=8,'gy'=2,'gz'=2] {'gx'}, dimensions={0}, use_global_device_ids=true | all-gather | bytes 73728 | tf_op jit(solution)/shard_map/all_gather | solution.py:93
  119.7 7.3 %copy.62 = bf16[8,8,2,64,128]{3,2,4,0,1:T(2,128)(2,1)} copy(bf16[8,8,2,64,128]{4,3,0,2,1:T(8,128)(2,1)S(1)} %bitcast.130) | data formatting | bytes 4194304 | tf_op jit(solution)/shard_map/all_to_all | solution.py:102
  127.0 6.8 %reshape.96 = bf16[64,128,8,16]{1,3,2,0:T(8,128)(2,1)S(1)} reshape(bf16[8,8,2,64,128]{3,2,4,1,0:T(2,128)(2,1)} %bitcast.125) | data formatting | bytes 4194304 | tf_op jit(solution)/shard_map/reshape | solution.py:36
  133.8 3.1 convert_bitcast_fusion.3
  136.9 8.2 %reshape.112 = bf16[64,2,64,128]{2,1,0,3:T(2,128)(2,1)} reshape(bf16[64,128,8,16]{1,0,3,2:T(8,128)(2,1)} %convert_bitcast_fusion.3) | data formatting | bytes 4194304 | tf_op jit(solution)/shard_map/convert_element_type | solution.py:103
  145.1 9.4 %copy.67 = bf16[64,2,64,128]{3,2,1,0:T(8,128)(2,1)} copy(bf16[64,2,64,128]{2,1,0,3:T(2,128)(2,1)} %reshape.112) | data formatting | bytes 4194304 | tf_op jit(solution)/shard_map/convert_element_type | solution.py:103
  154.5 4.6 %all-to-all-start.1 = ((bf16[64,2,64,128]{3,2,1,0:T(8,128)(2,1)}), bf16[64,2,64,128]{3,2,1,0:T(8,128)(2,1)S(1)}, u32[]{:S(2)}, u32[]{:S(2)}) async-start(bf16[64,2,64,128]{3,2,1,0:T(8,128)(2,1)} %copy.67), calls=%async_computation.1 | async-start | bytes 4194304 | tf_op jit(solution)/shard_map/all_to_all | solution.py:104
  159.2 84.0 %psum.22 = f32[16,256]{1,0:T(8,128)S(1)} all-reduce(f32[16,256]{1,0:T(8,128)S(1)} %reduce_sum.137), channel_id=1, replica_groups=mesh['gx'=8,'gy'=2,'gz'=2] {'gx','gz'}, use_global_device_ids=true, to_apply=%region_11.12 | all-reduce | flops 4096 | bytes 32768 | tf_op jit(solution)/shard_map/psum | solution.py:91
  243.2 4.6 %all_gather.10 = f32[32,256]{1,0:T(8,128)S(1)} all-gather(f32[16,256]{1,0:T(8,128)S(1)} %psum.22), channel_id=1, replica_groups=mesh['gx'=8,'gy'=2,'gz'=2] {'gy'}, dimensions={0}, use_global_device_ids=true | all-gather | bytes 49152 | tf_op jit(solution)/shard_map/all_gather | solution.py:94
  250.6 3.2 copy.68
  253.8 5.0 %convert_bitcast_fusion.1 = bf16[4,32,64,8,16]{2,1,4,0,3:T(8,128)(2,1)S(1)} fusion(bf16[4,32,64,8,16]{2,4,3,1,0:T(8,128)(2,1)} %bitcast.127, bf16[8,32,32,1,1]{1,0,2,4,3:T(8,128)(2,1)S(1)} %bitcast.138), kind=kOutput, calls=%fused_computation.52 | convolution fusion | flops 68157440 | bytes 4210688 | tf_op jit(solution)/shard_map/hab,xbmhd->xamhd/dot_general | solution.py:43
  258.8 3.5 copy.75
  262.3 4.8 %copy.76 = bf16[4,32,64,128]{3,2,0,1:T(8,128)(2,1)} copy(bf16[4,32,64,128]{2,3,1,0:T(8,128)(2,1)} %bitcast.128) | data formatting | bytes 4194304 | tf_op jit(solution)/shard_map/convert_element_type | solution.py:108
  267.1 3.8 all-to-all-start.2
  270.9 85.6 %psum.23 = bf16[64,256]{1,0:T(8,128)(2,1)S(1)} all-reduce(f32[64,256]{1,0:T(8,128)S(1)} %reduce_sum.140), channel_id=1, replica_groups=mesh['gx'=8,'gy'=2,'gz'=2] {'gx','gy'}, use_global_device_ids=true, to_apply=%region_15.16 | all-reduce | flops 16384 | bytes 98304 | tf_op jit(solution)/shard_map/psum | solution.py:92
  356.5 1.8 all_gather.11
  361.8 5.4 %all_to_all.81 = bf16[8,16,64,128]{3,2,1,0:T(8,128)(2,1)S(1)} all-to-all(bf16[8,16,64,128]{3,2,1,0:T(8,128)(2,1)S(1)} %bitcast.133), channel_id=1, replica_groups=mesh['gx'=8,'gy'=2,'gz'=2] {'gz'}, dimensions={0} | all-to-all | bytes 4194304 | tf_op jit(solution)/shard_map/all_to_all | solution.py:111
  367.2 7.3 %copy.79 = bf16[2,4,16,64,128]{3,0,4,2,1:T(2,128)(2,1)} copy(bf16[2,4,16,64,128]{4,3,2,1,0:T(8,128)(2,1)S(1)} %bitcast.131) | data formatting | bytes 4194304 | tf_op jit(solution)/shard_map/all_to_all | solution.py:111
  374.5 6.8 %reshape.104 = bf16[4,16,128,8,16]{2,4,3,1,0:T(8,128)(2,1)S(1)} reshape(bf16[4,16,2,64,128]{3,2,4,1,0:T(2,128)(2,1)} %bitcast.126) | data formatting | bytes 4194304 | tf_op jit(solution)/shard_map/reshape | solution.py:48
  382.6 3.0 copy.83
  385.6 6.6 %all_to_all.82 = bf16[4,16,128,128]{3,1,0,2:T(8,128)(2,1)S(1)} all-to-all(bf16[4,16,128,128]{3,1,0,2:T(8,128)(2,1)} %copy.83), channel_id=1, replica_groups=mesh['gx'=8,'gy'=2,'gz'=2] {'gz'}, dimensions={2} | all-to-all | bytes 4194304 | tf_op jit(solution)/shard_map/all_to_all | solution.py:113
  392.3 1.4 copy.85
  393.6 33.2 %while.27 = (s32[]{:T(128)}, bf16[8,16,64,128]{3,2,1,0:T(8,128)(2,1)}, bf16[8,16,64,128]{3,2,1,0:T(8,128)(2,1)}, bf16[8,16,64,128]{3,2,1,0:T(8,128)(2,1)S(1)}, b...) while((s32[]{:T(128)}, ...), condition=%wide.region_21.22_spmd, body=%wide.region_18.21_spmd.sunk | while | flops 442893312 | bytes 13308505 | solution.py:119
  (161 shorter events, 50.3 us)
Async XLA Ops:
  40.4 79.3 %all-to-all-start = ((bf16[8,16,64,128]{3,2,0,1:T(8,128)(2,1)}), bf16[8,16,64,128]{3,2,0,1:T(8,128)(2,1)S(1)}, u32[]{:S(2)}, u32[]{:S(2)}) async-start(bf16[8,16,64,128]{3,2,0,1:T(8,128)(2,1)} %get-tuple-element.82), calls=%async_computation | async-start | bytes 4194304 | tf_op jit(solution)/shard_map/all_to_all | solution.py:102
  154.5 96.1 %all-to-all-start.1 = ((bf16[64,2,64,128]{3,2,1,0:T(8,128)(2,1)}), bf16[64,2,64,128]{3,2,1,0:T(8,128)(2,1)S(1)}, u32[]{:S(2)}, u32[]{:S(2)}) async-start(bf16[64,2,64,128]{3,2,1,0:T(8,128)(2,1)} %copy.67), calls=%async_computation.1 | async-start | bytes 4194304 | tf_op jit(solution)/shard_map/all_to_all | solution.py:104
  267.1 94.5 %all-to-all-start.2 = ((bf16[4,32,64,128]{3,2,0,1:T(8,128)(2,1)}), bf16[4,32,64,128]{3,2,0,1:T(8,128)(2,1)S(1)}, u32[]{:S(2)}, u32[]{:S(2)}) async-start(bf16[4,32,64,128]{3,2,0,1:T(8,128)(2,1)} %copy.76), calls=%async_computation.2 | async-start | bytes 4194304 | tf_op jit(solution)/shard_map/all_to_all | solution.py:109
  392.2 1.4 copy-start
  392.2 1.4 copy-start.1
  392.2 1.4 copy-start.2
where the time goes:
time: 429 us; the launch traced here: 427 us
  blocking collectives  256 us (60%)
  local copies, waits for them, and re-layouts  83.2 us (19%)
  matrix products  38.9 us (9%)
  other arithmetic  27.4 us (6%)
  starting transfers between devices  15.7 us (4%)
  between operations  4.4 us (1%)
    psum x1, blocking collectives, body(): total_z = lax.psum(part_z, ('gx', 'gy'))  85.6 us
    psum x1, blocking collectives, body(): total_y = lax.psum(part_y, ('gx', 'gz'))  84 us
    all_gather x1, blocking collectives, body(): pooled_x = lax.all_gather(total_x, 'gx', axis=0, tiled=True)  61.6 us
    convert_element_type x2, local copies, waits for them, and re-layouts, body(): x_mixed = apply_first(kernel_x, lax.all_to_all(value, 'gx', split_axis=1,...  17.6 us
    reduce_sum x16, other arithmetic, norm_rows(): spread = jnp.mean(centred * centred, axis=-1, keepdims=True)  13.7 us
    dynamic_update_slice x40, local copies, waits for them, and re-layouts, body(): value, part_x, part_y, part_z = lax.map(project, tokens)  12.3 us
    dot_general x8, matrix products, project(): jnp.dot(normed.reshape(-1, width), w_qkv, preferred_element_type=jnp.floa...  11.8 us
    reduce_sum x8, other arithmetic, norm_rows(): mean = jnp.mean(values, axis=-1, keepdims=True)  9.28 us
  transfers between devices with their start and end apart: 3, of which 0 were waited for; matrix products, arithmetic and copies ran while one was open for 1% of the time, Pallas kernels for 0%

commit v1 on v0

v1 whole, which is shorter than its diff:
```python
import functools
import math

import jax
import jax.numpy as jnp
from jax import lax
from jax.experimental import pallas as pl
from jax.experimental.pallas import tpu as pltpu
from jax.sharding import PartitionSpec as P

HEADS = 8
EPS = 1e-05
VMEM_LIMIT = 56 * 1024 * 1024
F32 = jnp.float32
BF16 = jnp.bfloat16


def dot(a, b):
    return jnp.dot(a, b, preferred_element_type=F32)


def averaging(width):
    return jnp.full((width, width), 1.0 / width, BF16)


def head_mask(width, rank):
    shape = (HEADS, 1, width)
    lane = lax.broadcasted_iota(jnp.int32, shape, 2)
    return lane // rank == lax.broadcasted_iota(jnp.int32, shape, 0)


def spread_lanes(coef, out_ref, rank):
    width = coef.shape[-1]
    row = lax.broadcasted_iota(jnp.int32, (width, width), 0)
    lane = lax.broadcasted_iota(jnp.int32, (width, width), 1)
    same = row // rank == lane // rank
    for d in range(rank):
        pick = jnp.where(same & (row % rank == d), 1.0, 0.0).astype(BF16)
        out_ref[:, d, :] = dot(coef.astype(BF16), pick)


def project_kernel(lines, tok_ref, wv_ref, val_ref, pool_ref):
    step = pl.program_id(0)
    _, ny, nz, width = tok_ref.shape
    nx = pl.num_programs(0)

    @pl.when(step == 0)
    def _():
        pool_ref[...] = jnp.zeros_like(pool_ref)

    avg = averaging(width)
    tok = tok_ref[...].reshape(ny * nz, width)
    cent = tok.astype(F32) - dot(tok, avg)
    var = dot((cent * cent).astype(BF16), avg)
    normed = (cent * lax.rsqrt(var + EPS)).astype(BF16)
    val_ref[...] = dot(normed, wv_ref[...]).astype(BF16).reshape(val_ref.shape)
    full = normed.astype(F32).reshape(ny, nz, width)
    by_y = jnp.sum(full, axis=1)
    gx, gy, gz = (lax.axis_index(a) for a in ("gx", "gy", "gz"))
    rows_y = pl.ds(pl.multiple_of(lines[0] + gy * ny, 8), ny)
    rows_z = pl.ds(pl.multiple_of(lines[0] + lines[1] + gz * nz, 8), nz)
    pool_ref[pl.ds(gx * nx + step, 1), :] = jnp.sum(by_y, axis=0, keepdims=True)
    pool_ref[rows_y, :] += by_y
    pool_ref[rows_z, :] += jnp.sum(full, axis=0)


def coefficients(lines, pool, w_qk, out_ref):
    width = pool.shape[-1]
    rank = width // HEADS
    both = jnp.dot(pool, w_qk.astype(F32), precision=lax.Precision.HIGHEST)
    start = 0
    for length in lines:
        for part in range(2):
            cut = both[start : start + length, part * width : (part + 1) * width]
            total = jnp.sum(jnp.sum(cut * cut, axis=0, keepdims=True), axis=1, keepdims=True)
            unit = cut * lax.rsqrt(total / (length * width) + 1e-06)
            if part == 0:
                unit = unit * (1.0 / math.sqrt(rank * length))
            out_ref[start : start + length, part * width : (part + 1) * width] = unit
        start += length


def compress_kernel(lines, pool_ref, wqk_ref, val_ref, out_ref, coef_ref, key_y, key_z, state):
    _, ny, nz, width = val_ref.shape
    rank = width // HEADS

    @pl.when(pl.program_id(0) == 0)
    def _():
        coefficients(lines, pool_ref[...], wqk_ref[...], coef_ref)
        gy, gz = lax.axis_index("gy"), lax.axis_index("gz")
        rows_y = pl.ds(pl.multiple_of(lines[0] + gy * ny, 8), ny)
        rows_z = pl.ds(pl.multiple_of(lines[0] + lines[1] + gz * nz, 8), nz)
        spread_lanes(coef_ref[rows_y, width:], key_y, rank)
        key_z[...] = coef_ref[rows_z, width:].T.astype(BF16)

    mask = head_mask(width, rank)
    for y in range(ny):
        full = dot(key_z[...], val_ref[0, y]).reshape(HEADS, rank, width)
        state[y] = jnp.sum(jnp.where(mask, full, 0.0), axis=0)
    acc = jnp.zeros((rank, rank, width), F32)
    for y in range(ny):
        acc = acc + key_y[y][:, None, :] * state[y][None, :, :]
    out_ref[0] = acc.astype(out_ref.dtype)


def mix_x_kernel(line, coef_ref, in_ref, out_ref, query, key, mid):
    width = in_ref.shape[-1]
    rank = width // HEADS
    spread_lanes(coef_ref[:line, :width], query, rank)
    spread_lanes(coef_ref[:line, width:], key, rank)
    mid[...] = jnp.zeros_like(mid)

    def down(r, carry):
        mid[...] += key[r][:, None, :] * in_ref[r].astype(F32)[None, :, :]
        return carry

    lax.fori_loop(0, line, down, 0)

    def up(p, carry):
        out_ref[p] = jnp.sum(query[p][:, None, :] * mid[...], axis=0).astype(out_ref.dtype)
        return carry

    lax.fori_loop(0, line, up, 0)


def gelu(x):
    return 0.5 * x * (1.0 + jnp.tanh(math.sqrt(2.0 / math.pi) * (x + 0.044715 * (x * x * x))))


def finish_kernel(
    lines, coef_ref, in_ref, tok_ref, wo_ref, wgu_ref, wd_ref, out_ref, query_y, query_z, mixed
):
    _, ny, nz, width = tok_ref.shape
    rank = width // HEADS
    ff = wd_ref.shape[0]

    @pl.when(pl.program_id(0) == 0)
    def _():
        gy, gz = lax.axis_index("gy"), lax.axis_index("gz")
        rows_y = pl.ds(pl.multiple_of(lines[0] + gy * ny, 8), ny)
        rows_z = pl.ds(pl.multiple_of(lines[0] + lines[1] + gz * nz, 8), nz)
        spread_lanes(coef_ref[rows_y, :width], query_y, rank)
        query_z[...] = coef_ref[rows_z, :width].astype(BF16)

    mask = head_mask(width, rank)
    state = in_ref[0].astype(F32)
    avg = averaging(width)
    for y in range(ny):
        line = jnp.sum(query_y[y][:, None, :] * state, axis=0)
        wide = jnp.where(mask, line[None], 0.0).astype(BF16).reshape(HEADS * rank, width)
        mixed[y] = dot(query_z[...], wide).astype(BF16)
    group = 4
    for g in range(0, ny, group):
        rows = group * nz
        tok = tok_ref[0, g : g + group].reshape(rows, width).astype(F32)
        resid = tok + dot(mixed[g : g + group].reshape(rows, width), wo_ref[...])
        cent = resid - jnp.mean(resid, axis=-1, keepdims=True)
        var = dot((cent * cent).astype(BF16), avg)
        inner = (cent * lax.rsqrt(var + EPS)).astype(BF16)
        gate = dot(inner, wgu_ref[:, :ff])
        up = dot(inner, wgu_ref[:, ff:])
        hidden = (gelu(gate) * up).astype(BF16)
        result = resid + dot(hidden, wd_ref[...])
        out_ref[0, g : g + group] = result.astype(BF16).reshape(group, nz, width)


def whole(shape):
    return pl.BlockSpec(shape, lambda i: (0,) * len(shape))


def slab(shape):
    return pl.BlockSpec((1,) + shape[1:], lambda i: (i,) + (0,) * (len(shape) - 1))


def params(**more):
    return pltpu.CompilerParams(vmem_limit_bytes=VMEM_LIMIT, **more)


def body(tokens, w_qkv, w_out, w_gate_up, w_down):
    nx, ny, nz, width = tokens.shape
    rank = width // HEADS
    lines = (nx * lax.axis_size("gx"), ny * lax.axis_size("gy"), nz * lax.axis_size("gz"))
    total = sum(lines)
    w_qk, w_v = w_qkv[:, : 2 * width], w_qkv[:, 2 * width :]

    value, pool = pl.pallas_call(
        functools.partial(project_kernel, lines),
        grid=(nx,),
        in_specs=[slab(tokens.shape), whole(w_v.shape)],
        out_specs=[slab(tokens.shape), whole((total, width))],
        out_shape=[
            jax.ShapeDtypeStruct(tokens.shape, BF16),
            jax.ShapeDtypeStruct((total, width), F32),
        ],
        compiler_params=params(),
        name="project",
    )(tokens, w_v)
    pool = lax.psum(pool, ("gx", "gy", "gz"))

    small = (nx, rank, rank, width)
    state, coef = pl.pallas_call(
        functools.partial(compress_kernel, lines),
        grid=(nx,),
        in_specs=[whole(pool.shape), whole(w_qk.shape), slab(value.shape)],
        out_specs=[slab(small), whole((total, 2 * width))],
        out_shape=[
            jax.ShapeDtypeStruct(small, BF16),
            jax.ShapeDtypeStruct((total, 2 * width), F32),
        ],
        scratch_shapes=[
            pltpu.VMEM((ny, rank, width), F32),
            pltpu.VMEM((width, nz), BF16),
            pltpu.VMEM((ny, rank, width), F32),
        ],
        compiler_params=params(),
        name="compress",
    )(pool, w_qk, value)

    state = lax.psum_scatter(state, ("gy", "gz"), scatter_dimension=1, tiled=True)
    count_x = lax.axis_size("gx")
    part = state.reshape(nx, -1, width)
    part = lax.all_to_all(part, "gx", split_axis=1, concat_axis=0, tiled=True)
    part = pl.pallas_call(
        functools.partial(mix_x_kernel, lines[0]),
        out_shape=jax.ShapeDtypeStruct(part.shape, BF16),
        scratch_shapes=[
            pltpu.VMEM((lines[0], rank, width), F32),
            pltpu.VMEM((lines[0], rank, width), F32),
            pltpu.VMEM((rank,) + part.shape[1:], F32),
        ],
        compiler_params=params(),
        name="mix_x",
    )(coef, part)
    part = lax.all_to_all(part, "gx", split_axis=0, concat_axis=1, tiled=True)
    state = lax.all_gather(part.reshape(state.shape), ("gy", "gz"), axis=1, tiled=True)

    return pl.pallas_call(
        functools.partial(finish_kernel, lines),
        grid=(nx,),
        in_specs=[
            whole(coef.shape),
            slab(small),
            slab(tokens.shape),
            whole(w_out.shape),
            whole(w_gate_up.shape),
            whole(w_down.shape),
        ],
        out_specs=slab(tokens.shape),
        out_shape=jax.ShapeDtypeStruct(tokens.shape, BF16),
        scratch_shapes=[
            pltpu.VMEM((ny, rank, width), F32),
            pltpu.VMEM((nz, width), BF16),
            pltpu.VMEM((ny, nz, width), BF16),
        ],
        compiler_params=params(),
        name="finish",
    )(coef, state, tokens, w_out, w_gate_up, w_down)


def solution(mesh):
    in_specs = (P("gx", "gy", "gz", None), P(), P(), P(), P())
    out_specs = P("gx", "gy", "gz", None)
    return jax.shard_map(body, mesh=mesh, in_specs=in_specs, out_specs=out_specs, check_vma=False)
```

time: 429 us -> 252 us (0.59)
  blocking collectives: 256 us -> 30.3 us
  waiting for transfers between devices: 0.01 us -> 156 us
  local copies, waits for them, and re-layouts: 83.2 us -> 4.35 us
  Pallas kernels: 0 us -> 47 us
  matrix products: 38.9 us -> 0 us
  other arithmetic: 27.4 us -> 0 us
  starting transfers between devices: 15.7 us -> 0.04 us
  between operations: 4.4 us -> 14.1 us
    psum x3 -> x0, blocking collectives: 176 us -> none  [the longest x1 85.6 us: body(): total_z = lax.psum(part_z, ('gx', 'gy'))]
    psum x0 -> x1, waiting for transfers between devices: none -> 123 us  [body(): pool = lax.psum(pool, ('gx', 'gy', 'gz'))]
    all_gather x3 -> x1, blocking collectives: 68 us -> 6.98 us  [body(): lax.all_gather(part.reshape(state.shape), ('gy', 'gz'), axis=1, tiled=True)]
    pallas_call x0 -> x4, Pallas kernels: none -> 47 us  [the longest x1 26.3 us: body(): pl.pallas_call(functools.partial(finish_kernel, lines), grid=(nx,), in_sp...]
    dot_general x38 -> x0, matrix products: 38.9 us -> none  [the longest x8 11.8 us: project(): jnp.dot(normed.reshape(-1, width), w_qkv, preferred_element_type=jnp.floa...]
    unnamed x0 -> x3, waiting for transfers between devices: none -> 32.8 us
    convert_element_type x7 -> x0, local copies, waits for them, and re-layouts: 29.7 us -> none  [the longest x2 17.6 us: body(): x_mixed = apply_first(kernel_x, lax.all_to_all(value, 'gx', split_axis=1,...]
    reduce_sum x38 -> x0, other arithmetic: 27.2 us -> none  [the longest x16 13.7 us: norm_rows(): spread = jnp.mean(centred * centred, axis=-1, keepdims=True)]
  transfers between devices with their start and end apart: 3 -> 2, of which waited for: 0 -> 2; matrix products, arithmetic and copies ran while one was open for 1% -> 0% of each run, Pallas kernels for 0% -> 0%
where the time goes in v1:
time: 252 us; the launch traced here: 251 us
  waiting for transfers between devices  156 us (62%)
  Pallas kernels  47 us (19%)
  blocking collectives  30.3 us (12%)
  between operations  14.1 us (6%)
  local copies, waits for them, and re-layouts  4.35 us (2%)
    psum x1, waiting for transfers between devices, body(): pool = lax.psum(pool, ('gx', 'gy', 'gz'))  123 us
    unnamed x3, waiting for transfers between devices  32.8 us
    pallas_call x1, Pallas kernels, body(): pl.pallas_call(functools.partial(finish_kernel, lines), grid=(nx,), in_sp...  26.3 us
    all_to_all x1, blocking collectives, body(): part = lax.all_to_all(part, 'gx', split_axis=1, concat_axis=0, tiled=True)  12.7 us
    all_to_all x1, blocking collectives, body(): part = lax.all_to_all(part, 'gx', split_axis=0, concat_axis=1, tiled=True)  10.6 us
    pallas_call x1, Pallas kernels, body(): pl.pallas_call(functools.partial(compress_kernel, lines), grid=(nx,), in_...  7.93 us
    pallas_call x1, Pallas kernels, body(): pl.pallas_call(functools.partial(project_kernel, lines), grid=(nx,), in_s...  7.61 us
    all_gather x1, blocking collectives, body(): lax.all_gather(part.reshape(state.shape), ('gy', 'gz'), axis=1, tiled=True)  6.98 us
  transfers between devices with their start and end apart: 2, of which 2 were waited for; matrix products, arithmetic and copies ran while one was open for 0% of the time, Pallas kernels for 0%

profile of v1, /device:TPU:0, one launch (start us, length us, event | category | flops | bytes accessed | tf_op | source)
XLA Modules:
  0.0 251.4 jit_solution(10093014847881662994)
XLA Ops:
  6.5 0.0 copy-start
  6.5 0.0 all-reduce.4.cloned.1.call-start
  6.5 1.4 slice.6.wv_ref
  8.0 0.0 copy-start.1
  8.0 7.6 %project.1 = (bf16[8,16,64,128]{3,2,1,0:T(8,128)(2,1)}, f32[224,128]{1,0:T(8,128)}) custom-call(bf16[8,16,64,128]{3,2,1,0:T(8,128)(2,1)} %tok_ref.3, bf16[128,128]{1,0:T(8,128)(2,1)} %slice.6.wv_ref), custom_call_target="tpu_custom_call" | custom-call | tf_op jit(solution)/shard_map/project/pallas_call | solution.py:186
  15.6 0.0 all-reduce.4.cloned.1.call-update
  15.6 0.0 all-reduce.6.cloned.1.call-start
  15.7 0.0 copy-done
  15.7 0.6 slice.7.wqk_ref
  16.3 122.8 %all-reduce.4.cloned.1.call-done.pool_ref = f32[224,128]{1,0:T(8,128)} async-done(((f32[224,128]{1,0:T(8,128)}), f32[224,128]{1,0:T(8,128)}) %all-reduce.4.cloned.1.call-update) | async-done | bytes 114704 | tf_op jit(solution)/shard_map/psum | solution.py:198
  139.1 7.9 %compress.1 = (bf16[8,16,16,128]{3,2,1,0:T(8,128)(2,1)}, f32[224,256]{1,0:T(8,128)}) custom-call(f32[224,128]{1,0:T(8,128)} %all-reduce.4.cloned.1.call-done.pool_ref, bf16[128,256]{1,0:T(8,128)(2,1)} %slice.7.wqk_ref, bf16[8,16,64,128]{3,2,1,0:T(8,128)(2,1)} %get-tuple-element.10.val_ref), custom_call_target="tpu_custom_call" | custom-call | tf_op jit(solution)/shard_map/compress/pallas_call | solution.py:201
  147.1 0.0 all-reduce.6.cloned.1.call-update
  147.1 0.0 copy-done.1
  147.1 0.6 dynamic-slice
  148.3 32.8 %all-reduce.6.cloned.1.call-done = bf16[8,16,16,128]{3,2,1,0:T(8,128)(2,1)} async-done(((bf16[8,16,16,128]{3,2,1,0:T(8,128)(2,1)}), bf16[8,16,16,128]{3,2,1,0:T(8,128)(2,1)}) %all-reduce.6.cloned.1.call-update) | async-done | bytes 524304
  181.1 0.9 constant_dynamic-slice_fusion
  182.1 0.1 copy.9
  182.1 12.7 %all_to_all.33 = bf16[8,64,128]{2,0,1:T(8,128)(2,1)S(1)} all-to-all(bf16[8,64,128]{2,0,1:T(8,128)(2,1)S(1)} %copy.9), channel_id=1, replica_groups=mesh['gx'=8,'gy'=2,'gz'=2] {'gx'}, dimensions={1} | all-to-all | bytes 262144 | tf_op jit(solution)/shard_map/all_to_all | solution.py:222
  194.8 0.7 copy.11
  195.5 5.2 %mix_x.1 = bf16[64,8,128]{2,1,0:T(8,128)(2,1)} custom-call(f32[224,256]{1,0:T(8,128)} %get-tuple-element.11.coef_ref, bf16[64,8,128]{2,1,0:T(8,128)(2,1)} %bitcast.20), custom_call_target="tpu_custom_call" | custom-call | tf_op jit(solution)/shard_map/mix_x/pallas_call | solution.py:223
  200.7 10.6 %all_to_all.34 = bf16[64,8,128]{2,1,0:T(8,128)(2,1)S(1)} all-to-all(bf16[64,8,128]{2,1,0:T(8,128)(2,1)} %mix_x.1), channel_id=1, replica_groups=mesh['gx'=8,'gy'=2,'gz'=2] {'gx'}, dimensions={0} | all-to-all | bytes 262144 | tf_op jit(solution)/shard_map/all_to_all | solution.py:234
  211.3 7.0 %all_gather.3.in_ref = bf16[8,16,16,128]{3,2,1,0:T(8,128)(2,1)} all-gather(bf16[8,4,16,128]{3,2,1,0:T(8,128)(2,1)S(1)} %bitcast.16), channel_id=1, replica_groups=mesh['gx'=8,'gy'=2,'gz'=2] {'gy','gz'}, dimensions={1}, use_global_device_ids=true | all-gather | bytes 655360 | tf_op jit(solution)/shard_map/all_gather | solution.py:235
  218.3 26.3 %finish.1 = bf16[8,16,64,128]{3,2,1,0:T(8,128)(2,1)} custom-call(f32[224,256]{1,0:T(8,128)} %get-tuple-element.11.coef_ref, bf16[8,16,16,128]{3,2,1,0:T(8,128)(2,1)} %all_gather.3.in_ref, bf16[8,16,64,128]{3,2,1,0:T(8,128)(2,1)} %tok_ref.3, bf16[128,128]{1,0:T(8,128)(2,1)} %wo_ref.1, bf16[128,1024]{1,0:T(8,128)(2,1)} %wgu_ref.1, bf16[512,128]{1,0:T(8,128)(2,1)} %wd_ref.1), custom_call_target="tpu_custom_call" | custom-call | tf_op jit(solution)/shard_map/finish/pallas_call | solution.py:237
  (1 shorter events, 0.0 us)
Async XLA Ops:
  6.5 9.1 %copy-start = (bf16[128,384]{1,0:T(8,128)(2,1)S(1)}, bf16[128,384]{1,0:T(8,128)(2,1)}, u32[]{:S(2)}) copy-start(bf16[128,384]{1,0:T(8,128)(2,1)} %param.6) | copy-start | bytes 294916
  6.5 132.6 %all-reduce.4.cloned.1.call-start = ((), (), s32[]{:S(2)}) async-start(), calls=%async_computation.2 | async-start | bytes 229376 | tf_op jit(solution)/shard_map/psum | solution.py:198
  8.0 139.1 %copy-start.1 = (u32[32]{0:T(128)S(1)}, u32[32]{0:T(128)}, u32[]{:S(2)}) copy-start(u32[32]{0:T(128)} %constant.2) | copy-start | bytes 388
  15.6 165.5 %all-reduce.6.cloned.1.call-start = ((), (), s32[]{:S(2)}) async-start(), calls=%async_computation.3 | async-start | bytes 1048576
Sparse Core Ops, SparseCore 0:
  15.7 123.3 all-reduce.3
  147.2 33.8 all-reduce.5

commit v2 on v1

v2 whole, which is shorter than its diff:
```python
import functools
import math

import jax
import jax.numpy as jnp
from jax import lax
from jax.experimental import pallas as pl
from jax.experimental.pallas import tpu as pltpu
from jax.sharding import PartitionSpec as P

HEADS = 8
EPS = 1e-05
VMEM_LIMIT = 56 * 1024 * 1024
F32 = jnp.float32
BF16 = jnp.bfloat16


def dot(a, b):
    return jnp.dot(a, b, preferred_element_type=F32)


def averaging(width):
    return jnp.full((width, width), 1.0 / width, BF16)


def head_mask(width, rank):
    shape = (HEADS, 1, width)
    lane = lax.broadcasted_iota(jnp.int32, shape, 2)
    return lane // rank == lax.broadcasted_iota(jnp.int32, shape, 0)


def spread_lanes(coef, out_ref, rank):
    width = coef.shape[-1]
    row = lax.broadcasted_iota(jnp.int32, (width, width), 0)
    lane = lax.broadcasted_iota(jnp.int32, (width, width), 1)
    same = row // rank == lane // rank
    for d in range(rank):
        pick = jnp.where(same & (row % rank == d), 1.0, 0.0).astype(BF16)
        out_ref[:, d, :] = dot(coef.astype(BF16), pick)


def coefficients(lines, pool, w_qk, out_ref):
    width = pool.shape[-1]
    rank = width // HEADS
    both = jnp.dot(pool, w_qk.astype(F32), precision=lax.Precision.HIGHEST)
    start = 0
    for length in lines:
        for part in range(2):
            cut = both[start : start + length, part * width : (part + 1) * width]
            total = jnp.sum(jnp.sum(cut * cut, axis=0, keepdims=True), axis=1, keepdims=True)
            unit = cut * lax.rsqrt(total / (length * width) + 1e-06)
            if part == 0:
                unit = unit * (1.0 / math.sqrt(rank * length))
            out_ref[start : start + length, part * width : (part + 1) * width] = unit
        start += length


MESH = pl.DeviceIdType.MESH


def wait_bytes(view, sem):
    pltpu.make_async_copy(view, view, sem).wait()


def attend_kernel(
    sizes,
    lines,
    tok_ref,
    wqkv_ref,
    out_ref,
    coef_ref,
    value,
    pool_x,
    pool_y,
    pool_z,
    give,
    take,
    owned,
    spread,
    pooled,
    key_y,
    key_z,
    state,
    part_out,
    part_in,
    mine,
    x_out,
    x_in,
    query_x,
    key_x,
    mid,
    back_out,
    back_in,
    gathered,
    send,
    recv,
    back_recv,
):
    ci, cj, ck = sizes
    count = ci * cj * ck
    group = cj * ck
    nx, ny, nz, width = tok_ref.shape
    rank = width // HEADS
    gx, gy, gz = (lax.axis_index(a) for a in ("gx", "gy", "gz"))
    me = (gx * cj + gy) * ck + gz
    lane_of = gy * ck + gz

    def place(flat):
        return flat // group, flat // ck % cj, flat % ck

    barrier = pltpu.get_barrier_semaphore()

    def greet(off, carry):
        pl.semaphore_signal(
            barrier, inc=1, device_id=place(lax.rem(me + off, count)), device_id_type=MESH
        )
        return carry

    lax.fori_loop(1, count, greet, 0)

    avg = averaging(width)
    pool_y[...] = jnp.zeros_like(pool_y)
    pool_z[...] = jnp.zeros_like(pool_z)
    give[...] = jnp.zeros_like(give)

    def normalise(x, carry):
        tok = tok_ref[x].reshape(ny * nz, width)
        cent = tok.astype(F32) - dot(tok, avg)
        var = dot((cent * cent).astype(BF16), avg)
        normed = (cent * lax.rsqrt(var + EPS)).astype(BF16)
        value[x] = normed.reshape(ny, nz, width)
        full = normed.astype(F32).reshape(ny, nz, width)
        by_y = jnp.sum(full, axis=1)
        pool_x[pl.ds(x, 1), :] = jnp.sum(by_y, axis=0, keepdims=True)
        pool_y[...] += by_y
        pool_z[...] += jnp.sum(full, axis=0)
        return carry

    lax.fori_loop(0, nx, normalise, 0)

    held_x, held_y, held_z = -(-nx // group), -(-ny // (ci * ck)), -(-nz // (ci * cj))

    def starts(i, j, k):
        return (
            jnp.minimum((j * ck + k) * held_x, nx - held_x),
            jnp.minimum((i * ck + k) * held_y, ny - held_y),
            jnp.minimum((i * cj + j) * held_z, nz - held_z),
        )

    def fill(s, carry):
        at_x, at_y, at_z = starts(*place(s))
        for r in range(held_x):
            give[s, r : r + 1, :] = pool_x[pl.ds(at_x + r, 1), :]
        for r in range(held_y):
            give[s, held_x + r : held_x + r + 1, :] = pool_y[pl.ds(at_y + r, 1), :]
        for r in range(held_z):
            row = held_x + held_y + r
            give[s, row : row + 1, :] = pool_z[pl.ds(at_z + r, 1), :]
        return carry

    lax.fori_loop(0, count, fill, 0)
    pl.semaphore_wait(barrier, count - 1)

    def send_rows(off, carry):
        to = lax.rem(me + off, count)
        pltpu.make_async_remote_copy(
            give.at[to], take.at[me], send.at[0], recv.at[0], device_id=place(to), device_id_type=MESH
        ).start()
        return carry

    lax.fori_loop(1, count, send_rows, 0)
    take[me] = give[me]

    def project(x, carry):
        normed = value[x].reshape(ny * nz, width)
        value[x] = dot(normed, wqkv_ref[:, 2 * width :]).astype(BF16).reshape(ny, nz, width)
        return carry

    lax.fori_loop(0, nx, project, 0)
    wait_bytes(take.at[pl.ds(0, count - 1)], recv.at[0])

    row = lax.broadcasted_iota(jnp.int32, owned.shape, 0)

    def add_rows(s, acc):
        i, j, k = place(s)
        ours = jnp.where(
            row < held_x,
            (i == gx).astype(jnp.int32),
            jnp.where(row < held_x + held_y, (j == gy).astype(jnp.int32), (k == gz).astype(jnp.int32)),
        )
        return acc + jnp.where(ours > 0, take[s], 0.0)

    owned[...] = lax.fori_loop(0, count, add_rows, jnp.zeros(owned.shape, F32))

    def send_owned(off, carry):
        to = lax.rem(me + off, count)
        pltpu.make_async_remote_copy(
            owned, spread.at[me], send.at[1], recv.at[1], device_id=place(to), device_id_type=MESH
        ).start()
        return carry

    lax.fori_loop(1, count, send_owned, 0)
    spread[me] = owned[...]
    wait_bytes(spread.at[pl.ds(0, count - 1)], recv.at[1])

    def unfold(s, carry):
        i, j, k = place(s)
        at_x, at_y, at_z = starts(i, j, k)
        for r in range(held_x):
            pooled[pl.ds(i * nx + at_x + r, 1), :] = spread[s, r : r + 1, :]
        for r in range(held_y):
            pooled[pl.ds(lines[0] + j * ny + at_y + r, 1), :] = spread[s, held_x + r : held_x + r + 1, :]
        for r in range(held_z):
            row = held_x + held_y + r
            pooled[pl.ds(lines[0] + lines[1] + k * nz + at_z + r, 1), :] = spread[s, row : row + 1, :]
        return carry

    lax.fori_loop(0, count, unfold, 0)
    coefficients(lines, pooled[...], wqkv_ref[:, : 2 * width], coef_ref)

    rows_y = pl.ds(pl.multiple_of(lines[0] + gy * ny, 8), ny)
    rows_z = pl.ds(pl.multiple_of(lines[0] + lines[1] + gz * nz, 8), nz)
    spread_lanes(coef_ref[rows_y, width:], key_y, rank)
    key_z[...] = coef_ref[rows_z, width:].T.astype(BF16)
    mask = head_mask(width, rank)
    share = rank // group

    def compress(x, carry):
        for y in range(ny):
            full = dot(key_z[...], value[x, y]).reshape(HEADS, rank, width)
            state[y] = jnp.sum(jnp.where(mask, full, 0.0), axis=0)
        acc = jnp.zeros((rank, rank, width), F32)
        for y in range(ny):
            acc = acc + key_y[y][:, None, :] * state[y][None, :, :]
        part_out[x] = acc.astype(BF16)

        def send_share(off, carry):
            to = lax.rem(lane_of + off, group)
            pltpu.make_async_remote_copy(
                part_out.at[x, pl.ds(to * share, share)],
                part_in.at[lane_of, x],
                send.at[2],
                recv.at[2],
                device_id=(gx, to // ck, to % ck),
                device_id_type=MESH,
            ).start()
            return carry

        lax.fori_loop(1, group, send_share, 0)
        part_in[lane_of, x] = part_out[x, pl.ds(lane_of * share, share)]
        return carry

    lax.fori_loop(0, nx, compress, 0)
    spread_lanes(coef_ref[: lines[0], :width], query_x, rank)
    spread_lanes(coef_ref[: lines[0], width:], key_x, rank)
    wait_bytes(part_in.at[pl.ds(0, group - 1)], recv.at[2])

    rows = share * rank // ci
    total = jnp.zeros((nx, share, rank, width), F32)
    for g in range(group):
        total = total + part_in[g].astype(F32)
    mine[...] = total.reshape(nx, share * rank, width)
    for p in range(ci):
        x_out[p] = mine[:, p * rows : (p + 1) * rows, :].reshape(nx * rows, width).astype(BF16)

    def send_x(off, carry):
        to = lax.rem(gx + off, ci)
        pltpu.make_async_remote_copy(
            x_out.at[to], x_in.at[gx], send.at[3], recv.at[3], device_id=(to, gy, gz), device_id_type=MESH
        ).start()
        return carry

    lax.fori_loop(1, ci, send_x, 0)
    x_in[gx] = x_out[gx]
    wait_bytes(x_in.at[pl.ds(0, ci - 1)], recv.at[3])

    mid[...] = jnp.zeros_like(mid)

    def down(i, carry):
        block = x_in[i].astype(F32).reshape(nx, rows, width)
        acc = mid[...]
        for x in range(nx):
            acc = acc + key_x[i * nx + x][:, None, :] * block[x][None]
        mid[...] = acc
        return carry

    lax.fori_loop(0, ci, down, 0)

    def up(off, carry):
        to = lax.rem(gx + off, ci)
        line = [jnp.sum(query_x[to * nx + x][:, None, :] * mid[...], axis=0) for x in range(nx)]
        back_out[to] = jnp.concatenate(line, axis=0).astype(BF16)
        return carry

    def up_send(off, carry):
        up(off, carry)
        to = lax.rem(gx + off, ci)
        pltpu.make_async_remote_copy(
            back_out.at[to],
            back_in.at[gx],
            send.at[4],
            back_recv.at[gx],
            device_id=(to, gy, gz),
            device_id_type=MESH,
        ).start()
        return carry

    lax.fori_loop(1, ci, up_send, 0)
    up(0, 0)
    back_in[gx] = back_out[gx]

    def forward(chunk):
        def send_chunk(other, carry):
            to = lax.rem(lane_of + other, group)
            pltpu.make_async_remote_copy(
                back_in.at[chunk],
                gathered.at[lane_of, chunk],
                send.at[5],
                recv.at[5],
                device_id=(gx, to // ck, to % ck),
                device_id_type=MESH,
            ).start()
            return carry

        lax.fori_loop(1, group, send_chunk, 0)
        gathered[lane_of, chunk] = back_in[chunk]

    forward(gx)

    def arrive(off, carry):
        chunk = lax.rem(gx + ci - off, ci)
        wait_bytes(back_in.at[chunk], back_recv.at[chunk])
        forward(chunk)
        return carry

    lax.fori_loop(1, ci, arrive, 0)
    wait_bytes(gathered.at[pl.ds(0, group - 1)], recv.at[5])
    for g in range(group):
        for q in range(ci):
            at = (g * ci + q) * rows
            out_ref[:, at : at + rows, :] = gathered[g, q].astype(F32).reshape(nx, rows, width)

    wait_bytes(give.at[pl.ds(0, count - 1)], send.at[0])
    wait_bytes(spread.at[pl.ds(0, count - 1)], send.at[1])
    wait_bytes(part_in.at[pl.ds(0, group - 1)], send.at[2])
    wait_bytes(x_out.at[pl.ds(0, ci - 1)], send.at[3])
    wait_bytes(back_out.at[pl.ds(0, ci - 1)], send.at[4])
    wait_bytes(gathered.at[pl.ds(0, group - 1)], send.at[5])


def gelu(x):
    return 0.5 * x * (1.0 + jnp.tanh(math.sqrt(2.0 / math.pi) * (x + 0.044715 * (x * x * x))))


def finish_kernel(
    lines, coef_ref, in_ref, tok_ref, wo_ref, wgu_ref, wd_ref, out_ref, query_y, query_z, mixed
):
    _, ny, nz, width = tok_ref.shape
    rank = width // HEADS
    ff = wd_ref.shape[0]

    @pl.when(pl.program_id(0) == 0)
    def _():
        gy, gz = lax.axis_index("gy"), lax.axis_index("gz")
        rows_y = pl.ds(pl.multiple_of(lines[0] + gy * ny, 8), ny)
        rows_z = pl.ds(pl.multiple_of(lines[0] + lines[1] + gz * nz, 8), nz)
        spread_lanes(coef_ref[rows_y, :width], query_y, rank)
        query_z[...] = coef_ref[rows_z, :width].astype(BF16)

    mask = head_mask(width, rank)
    state = in_ref[0].reshape(rank, rank, width)
    avg = averaging(width)
    for y in range(ny):
        line = jnp.sum(query_y[y][:, None, :] * state, axis=0)
        wide = jnp.where(mask, line[None], 0.0).astype(BF16).reshape(HEADS * rank, width)
        mixed[y] = dot(query_z[...], wide).astype(BF16)
    group = 4
    for g in range(0, ny, group):
        rows = group * nz
        tok = tok_ref[0, g : g + group].reshape(rows, width).astype(F32)
        resid = tok + dot(mixed[g : g + group].reshape(rows, width), wo_ref[...])
        cent = resid - jnp.mean(resid, axis=-1, keepdims=True)
        var = dot((cent * cent).astype(BF16), avg)
        inner = (cent * lax.rsqrt(var + EPS)).astype(BF16)
        gate = dot(inner, wgu_ref[:, :ff])
        up = dot(inner, wgu_ref[:, ff:])
        hidden = (gelu(gate) * up).astype(BF16)
        result = resid + dot(hidden, wd_ref[...])
        out_ref[0, g : g + group] = result.astype(BF16).reshape(group, nz, width)


def whole(shape):
    return pl.BlockSpec(shape, lambda i: (0,) * len(shape))


def slab(shape):
    return pl.BlockSpec((1,) + shape[1:], lambda i: (i,) + (0,) * (len(shape) - 1))


def params(**more):
    return pltpu.CompilerParams(vmem_limit_bytes=VMEM_LIMIT, **more)


def body(tokens, w_qkv, w_out, w_gate_up, w_down):
    nx, ny, nz, width = tokens.shape
    rank = width // HEADS
    lines = (nx * lax.axis_size("gx"), ny * lax.axis_size("gy"), nz * lax.axis_size("gz"))
    total = sum(lines)
    sizes = tuple(lax.axis_size(a) for a in ("gx", "gy", "gz"))
    count, group = math.prod(sizes), sizes[1] * sizes[2]
    held = -(-nx // group) - (-ny // (sizes[0] * sizes[2])) - (-nz // (sizes[0] * sizes[1]))
    held = -(-held // 8) * 8
    share = rank // group
    rows = share * rank // sizes[0]
    small = (nx, rank * rank, width)
    state, coef = pl.pallas_call(
        functools.partial(attend_kernel, sizes, lines),
        in_specs=[pl.BlockSpec(memory_space=pltpu.VMEM)] * 2,
        out_specs=[pl.BlockSpec(memory_space=pltpu.VMEM)] * 2,
        out_shape=[
            jax.ShapeDtypeStruct(small, F32),
            jax.ShapeDtypeStruct((total, 2 * width), F32),
        ],
        scratch_shapes=[
            pltpu.VMEM(tokens.shape, BF16),
            pltpu.VMEM((nx, width), F32),
            pltpu.VMEM((ny, width), F32),
            pltpu.VMEM((nz, width), F32),
            pltpu.VMEM((count, held, width), F32),
            pltpu.VMEM((count, held, width), F32),
            pltpu.VMEM((held, width), F32),
            pltpu.VMEM((count, held, width), F32),
            pltpu.VMEM((total, width), F32),
            pltpu.VMEM((ny, rank, width), F32),
            pltpu.VMEM((width, nz), BF16),
            pltpu.VMEM((ny, rank, width), F32),
            pltpu.VMEM((nx, rank, rank, width), BF16),
            pltpu.VMEM((group, nx, share, rank, width), BF16),
            pltpu.VMEM((nx, share * rank, width), F32),
            pltpu.VMEM((sizes[0], nx * rows, width), BF16),
            pltpu.VMEM((sizes[0], nx * rows, width), BF16),
            pltpu.VMEM((lines[0], rank, width), F32),
            pltpu.VMEM((lines[0], rank, width), F32),
            pltpu.VMEM((rank, rows, width), F32),
            pltpu.VMEM((sizes[0], nx * rows, width), BF16),
            pltpu.VMEM((sizes[0], nx * rows, width), BF16),
            pltpu.VMEM((group, sizes[0], nx * rows, width), BF16),
            pltpu.SemaphoreType.DMA((6,)),
            pltpu.SemaphoreType.DMA((6,)),
            pltpu.SemaphoreType.DMA((sizes[0],)),
        ],
        compiler_params=params(collective_id=0, has_side_effects=True),
        name="attend",
    )(tokens, w_qkv)

    return pl.pallas_call(
        functools.partial(finish_kernel, lines),
        grid=(nx,),
        in_specs=[
            whole(coef.shape),
            slab(small),
            slab(tokens.shape),
            whole(w_out.shape),
            whole(w_gate_up.shape),
            whole(w_down.shape),
        ],
        out_specs=slab(tokens.shape),
        out_shape=jax.ShapeDtypeStruct(tokens.shape, BF16),
        scratch_shapes=[
            pltpu.VMEM((ny, rank, width), F32),
            pltpu.VMEM((nz, width), BF16),
            pltpu.VMEM((ny, nz, width), BF16),
        ],
        compiler_params=params(),
        name="finish",
    )(coef, state, tokens, w_out, w_gate_up, w_down)


def solution(mesh):
    in_specs = (P("gx", "gy", "gz", None), P(), P(), P(), P())
    out_specs = P("gx", "gy", "gz", None)
    return jax.shard_map(body, mesh=mesh, in_specs=in_specs, out_specs=out_specs, check_vma=False)
```

time: 252 us -> 73.6 us (0.29)
  waiting for transfers between devices: 156 us -> 0 us
  blocking collectives: 30.3 us -> 0 us
  Pallas kernels: 47 us -> 73.5 us
  between operations: 14.1 us -> 0.01 us
  local copies, waits for them, and re-layouts: 4.35 us -> 0 us
    psum x1 -> x0, waiting for transfers between devices: 123 us -> none  [body(): pool = lax.psum(pool, ('gx', 'gy', 'gz'))]
    unnamed x3 -> x0, waiting for transfers between devices: 32.8 us -> none
    pallas_call x3 -> x1, Pallas kernels: 20.7 us -> 47.1 us  [body(): pl.pallas_call(functools.partial(attend_kernel, sizes, lines), in_specs=[...]
    all_to_all x2 -> x0, blocking collectives: 23.3 us -> none  [the longest x1 12.7 us: body(): part = lax.all_to_all(part, 'gx', split_axis=1, concat_axis=0, tiled=True)]
    all_gather x1 -> x0, blocking collectives: 6.98 us -> none  [body(): lax.all_gather(part.reshape(state.shape), ('gy', 'gz'), axis=1, tiled=True)]
  transfers between devices with their start and end apart: 2 -> 0, of which waited for: 2 -> 0; matrix products, arithmetic and copies ran while one was open for 0% -> 0% of each run, Pallas kernels for 0% -> 0%
where the time goes in v2:
time: 73.6 us; the launch traced here: 73.5 us
  Pallas kernels  73.5 us (100%)
    pallas_call x1, Pallas kernels, body(): pl.pallas_call(functools.partial(attend_kernel, sizes, lines), in_specs=[...  47.1 us
    pallas_call x1, Pallas kernels, body(): pl.pallas_call(functools.partial(finish_kernel, lines), grid=(nx,), in_sp...  26.4 us

profile of v2, /device:TPU:0, one launch (start us, length us, event | category | flops | bytes accessed | tf_op | source)
XLA Modules:
  0.0 73.5 jit_solution(14850791535346663391)
XLA Ops:
  0.0 47.1 %attend.1 = (f32[8,256,128]{2,1,0:T(8,128)}, f32[224,256]{1,0:T(8,128)}) custom-call(bf16[8,16,64,128]{3,2,1,0:T(8,128)(2,1)} %tok_ref.3, bf16[128,384]{1,0:T(8,128)(2,1)} %wqkv_ref.1), custom_call_target="tpu_custom_call" | custom-call | tf_op jit(solution)/shard_map/attend/pallas_call | solution.py:416
  47.1 26.4 %finish.1 = bf16[8,16,64,128]{3,2,1,0:T(8,128)(2,1)} custom-call(f32[224,256]{1,0:T(8,128)} %get-tuple-element.7.coef_ref, f32[8,256,128]{2,1,0:T(8,128)} %get-tuple-element.8.in_ref, bf16[8,16,64,128]{3,2,1,0:T(8,128)(2,1)} %tok_ref.3, bf16[128,128]{1,0:T(8,128)(2,1)} %wo_ref.1, bf16[128,1024]{1,0:T(8,128)(2,1)} %wgu_ref.1, bf16[512,128]{1,0:T(8,128)(2,1)} %wd_ref.1), custom_call_target="tpu_custom_call" | custom-call | tf_op jit(solution)/shard_map/finish/pallas_call | solution.py:456

commit v3 on v2

--- a/solution.py
+++ b/solution.py
@@ -36,7 +36,7 @@
     same = row // rank == lane // rank
     for d in range(rank):
         pick = jnp.where(same & (row % rank == d), 1.0, 0.0).astype(BF16)
-        out_ref[:, d, :] = dot(coef.astype(BF16), pick)
+        out_ref[d] = dot(coef.astype(BF16), pick)
 
 
 def coefficients(lines, pool, w_qk, out_ref):
@@ -226,12 +226,14 @@
     share = rank // group
 
     def compress(x, carry):
-        for y in range(ny):
-            full = dot(key_z[...], value[x, y]).reshape(HEADS, rank, width)
-            state[y] = jnp.sum(jnp.where(mask, full, 0.0), axis=0)
+        for y in range(0, ny, 2):
+            pair = dot(key_z[...], jnp.concatenate([value[x, y], value[x, y + 1]], axis=1))
+            for e in range(2):
+                full = pair[:, e * width : (e + 1) * width].reshape(HEADS, rank, width)
+                state[y + e] = jnp.sum(jnp.where(mask, full, 0.0), axis=0)
         acc = jnp.zeros((rank, rank, width), F32)
         for y in range(ny):
-            acc = acc + key_y[y][:, None, :] * state[y][None, :, :]
+            acc = acc + key_y[:, y : y + 1, :] * state[y][None, :, :]
         part_out[x] = acc.astype(BF16)
 
         def send_share(off, carry):
@@ -280,7 +282,7 @@
         block = x_in[i].astype(F32).reshape(nx, rows, width)
         acc = mid[...]
         for x in range(nx):
-            acc = acc + key_x[i * nx + x][:, None, :] * block[x][None]
+            acc = acc + key_x[:, pl.ds(i * nx + x, 1), :] * block[x][None]
         mid[...] = acc
         return carry
 
@@ -288,7 +290,7 @@
 
     def up(off, carry):
         to = lax.rem(gx + off, ci)
-        line = [jnp.sum(query_x[to * nx + x][:, None, :] * mid[...], axis=0) for x in range(nx)]
+        line = [jnp.sum(query_x[:, pl.ds(to * nx + x, 1), :] * mid[...], axis=0) for x in range(nx)]
         back_out[to] = jnp.concatenate(line, axis=0).astype(BF16)
         return carry
 
@@ -348,8 +350,11 @@
     wait_bytes(gathered.at[pl.ds(0, group - 1)], send.at[5])
 
 
-def gelu(x):
-    return 0.5 * x * (1.0 + jnp.tanh(math.sqrt(2.0 / math.pi) * (x + 0.044715 * (x * x * x))))
+def twice_gelu_times(x, up):
+    scale = math.sqrt(2.0 / math.pi)
+    tanh = jnp.tanh(x * (x * x * jnp.array(scale * 0.044715, x.dtype) + jnp.array(scale, x.dtype)))
+    both = x * up
+    return both * tanh + both
 
 
 def finish_kernel(
@@ -367,25 +372,30 @@
         spread_lanes(coef_ref[rows_y, :width], query_y, rank)
         query_z[...] = coef_ref[rows_z, :width].astype(BF16)
 
-    mask = head_mask(width, rank)
+    mask = jnp.broadcast_to(jnp.where(head_mask(width, rank), 1.0, 0.0), (HEADS, rank, width)).astype(BF16)
     state = in_ref[0].reshape(rank, rank, width)
     avg = averaging(width)
-    for y in range(ny):
-        line = jnp.sum(query_y[y][:, None, :] * state, axis=0)
-        wide = jnp.where(mask, line[None], 0.0).astype(BF16).reshape(HEADS * rank, width)
-        mixed[y] = dot(query_z[...], wide).astype(BF16)
+    for y in range(0, ny, 2):
+        wide = []
+        for e in range(2):
+            line = jnp.sum(query_y[:, y + e : y + e + 1, :] * state, axis=0).astype(BF16)
+            wide.append((mask * line[None]).reshape(HEADS * rank, width))
+        pair = dot(query_z[...], jnp.concatenate(wide, axis=1)).astype(BF16)
+        mixed[y] = pair[:, :width]
+        mixed[y + 1] = pair[:, width:]
     group = 4
     for g in range(0, ny, group):
         rows = group * nz
         tok = tok_ref[0, g : g + group].reshape(rows, width).astype(F32)
         resid = tok + dot(mixed[g : g + group].reshape(rows, width), wo_ref[...])
-        cent = resid - jnp.mean(resid, axis=-1, keepdims=True)
+        high = resid.astype(BF16)
+        low = (resid - high.astype(F32)).astype(BF16)
+        cent = resid - (dot(high, avg) + dot(low, avg))
         var = dot((cent * cent).astype(BF16), avg)
         inner = (cent * lax.rsqrt(var + EPS)).astype(BF16)
-        gate = dot(inner, wgu_ref[:, :ff])
-        up = dot(inner, wgu_ref[:, ff:])
-        hidden = (gelu(gate) * up).astype(BF16)
-        result = resid + dot(hidden, wd_ref[...])
+        gate = dot(inner, wgu_ref[:, :ff]).astype(BF16)
+        up = dot(inner, wgu_ref[:, ff:]).astype(BF16)
+        result = resid + 0.5 * dot(twice_gelu_times(gate, up), wd_ref[...])
         out_ref[0, g : g + group] = result.astype(BF16).reshape(group, nz, width)
 
 
@@ -431,7 +441,7 @@
             pltpu.VMEM((held, width), F32),
             pltpu.VMEM((count, held, width), F32),
             pltpu.VMEM((total, width), F32),
-            pltpu.VMEM((ny, rank, width), F32),
+            pltpu.VMEM((rank, ny, width), F32),
             pltpu.VMEM((width, nz), BF16),
             pltpu.VMEM((ny, rank, width), F32),
             pltpu.VMEM((nx, rank, rank, width), BF16),
@@ -439,8 +449,8 @@
             pltpu.VMEM((nx, share * rank, width), F32),
             pltpu.VMEM((sizes[0], nx * rows, width), BF16),
             pltpu.VMEM((sizes[0], nx * rows, width), BF16),
-            pltpu.VMEM((lines[0], rank, width), F32),
-            pltpu.VMEM((lines[0], rank, width), F32),
+            pltpu.VMEM((rank, lines[0], width), F32),
+            pltpu.VMEM((rank, lines[0], width), F32),
             pltpu.VMEM((rank, rows, width), F32),
             pltpu.VMEM((sizes[0], nx * rows, width), BF16),
             pltpu.VMEM((sizes[0], nx * rows, width), BF16),
@@ -467,7 +477,7 @@
         out_specs=slab(tokens.shape),
         out_shape=jax.ShapeDtypeStruct(tokens.shape, BF16),
         scratch_shapes=[
-            pltpu.VMEM((ny, rank, width), F32),
+            pltpu.VMEM((rank, ny, width), F32),
             pltpu.VMEM((nz, width), BF16),
             pltpu.VMEM((ny, nz, width), BF16),
         ],

time: 73.6 us -> 74.2 us (level)
    pallas_call x1, Pallas kernels: 26.4 us -> 27.3 us  [body(): pl.pallas_call(functools.partial(finish_kernel, lines), grid=(nx,), in_sp...]
where the time goes in v3:
time: 74.2 us; the launch traced here: 74.1 us
  Pallas kernels  74 us (100%)
    pallas_call x1, Pallas kernels, body(): pl.pallas_call(functools.partial(attend_kernel, sizes, lines), in_specs=[...  46.7 us
    pallas_call x1, Pallas kernels, body(): pl.pallas_call(functools.partial(finish_kernel, lines), grid=(nx,), in_sp...  27.3 us

profile of v3, /device:TPU:0, one launch (start us, length us, event | category | flops | bytes accessed | tf_op | source)
XLA Modules:
  0.0 74.1 jit_solution(5754567091706936901)
XLA Ops:
  0.0 46.7 %attend.1 = (f32[8,256,128]{2,1,0:T(8,128)}, f32[224,256]{1,0:T(8,128)}) custom-call(bf16[8,16,64,128]{3,2,1,0:T(8,128)(2,1)} %tok_ref.3, bf16[128,384]{1,0:T(8,128)(2,1)} %wqkv_ref.1), custom_call_target="tpu_custom_call" | custom-call | tf_op jit(solution)/shard_map/attend/pallas_call | solution.py:426
  46.7 27.3 %finish.1 = bf16[8,16,64,128]{3,2,1,0:T(8,128)(2,1)} custom-call(f32[224,256]{1,0:T(8,128)} %get-tuple-element.7.coef_ref, f32[8,256,128]{2,1,0:T(8,128)} %get-tuple-element.8.in_ref, bf16[8,16,64,128]{3,2,1,0:T(8,128)(2,1)} %tok_ref.3, bf16[128,128]{1,0:T(8,128)(2,1)} %wo_ref.1, bf16[128,1024]{1,0:T(8,128)(2,1)} %wgu_ref.1, bf16[512,128]{1,0:T(8,128)(2,1)} %wd_ref.1), custom_call_target="tpu_custom_call" | custom-call | tf_op jit(solution)/shard_map/finish/pallas_call | solution.py:466

commit v4 on v3

--- a/solution.py
+++ b/solution.py
@@ -95,6 +95,7 @@
     send,
     recv,
     back_recv,
+    cross_recv,
 ):
     ci, cj, ck = sizes
     count = ci * cj * ck
@@ -106,7 +107,7 @@
     lane_of = gy * ck + gz
 
     def place(flat):
-        return flat // group, flat // ck % cj, flat % ck
+        return lax.div(flat, group), lax.rem(lax.div(flat, ck), cj), lax.rem(flat, ck)
 
     barrier = pltpu.get_barrier_semaphore()
 
@@ -123,17 +124,23 @@
     pool_z[...] = jnp.zeros_like(pool_z)
     give[...] = jnp.zeros_like(give)
 
+    piece = 4
+
     def normalise(x, carry):
-        tok = tok_ref[x].reshape(ny * nz, width)
-        cent = tok.astype(F32) - dot(tok, avg)
-        var = dot((cent * cent).astype(BF16), avg)
-        normed = (cent * lax.rsqrt(var + EPS)).astype(BF16)
-        value[x] = normed.reshape(ny, nz, width)
-        full = normed.astype(F32).reshape(ny, nz, width)
-        by_y = jnp.sum(full, axis=1)
+        by_y, by_z = [], jnp.zeros((nz, width), F32)
+        for y in range(0, ny, piece):
+            tok = tok_ref[x, y : y + piece].reshape(piece * nz, width)
+            cent = tok.astype(F32) - dot(tok, avg)
+            var = dot((cent * cent).astype(BF16), avg)
+            normed = (cent * lax.rsqrt(var + EPS)).astype(BF16)
+            value[x, y : y + piece] = normed.reshape(piece, nz, width)
+            full = normed.astype(F32).reshape(piece, nz, width)
+            by_y.append(jnp.sum(full, axis=1))
+            by_z = by_z + jnp.sum(full, axis=0)
+        by_y = jnp.concatenate(by_y, axis=0)
         pool_x[pl.ds(x, 1), :] = jnp.sum(by_y, axis=0, keepdims=True)
         pool_y[...] += by_y
-        pool_z[...] += jnp.sum(full, axis=0)
+        pool_z[...] += by_z
         return carry
 
     lax.fori_loop(0, nx, normalise, 0)
@@ -158,7 +165,7 @@
             give[s, row : row + 1, :] = pool_z[pl.ds(at_z + r, 1), :]
         return carry
 
-    lax.fori_loop(0, count, fill, 0)
+    lax.fori_loop(0, count, fill, 0, unroll=4)
     pl.semaphore_wait(barrier, count - 1)
 
     def send_rows(off, carry):
@@ -168,7 +175,7 @@
         ).start()
         return carry
 
-    lax.fori_loop(1, count, send_rows, 0)
+    lax.fori_loop(1, count, send_rows, 0, unroll=4)
     take[me] = give[me]
 
     def project(x, carry):
@@ -190,7 +197,7 @@
         )
         return acc + jnp.where(ours > 0, take[s], 0.0)
 
-    owned[...] = lax.fori_loop(0, count, add_rows, jnp.zeros(owned.shape, F32))
+    owned[...] = lax.fori_loop(0, count, add_rows, jnp.zeros(owned.shape, F32), unroll=4)
 
     def send_owned(off, carry):
         to = lax.rem(me + off, count)
@@ -199,7 +206,7 @@
         ).start()
         return carry
 
-    lax.fori_loop(1, count, send_owned, 0)
+    lax.fori_loop(1, count, send_owned, 0, unroll=4)
     spread[me] = owned[...]
     wait_bytes(spread.at[pl.ds(0, count - 1)], recv.at[1])
 
@@ -215,7 +222,7 @@
             pooled[pl.ds(lines[0] + lines[1] + k * nz + at_z + r, 1), :] = spread[s, row : row + 1, :]
         return carry
 
-    lax.fori_loop(0, count, unfold, 0)
+    lax.fori_loop(0, count, unfold, 0, unroll=4)
     coefficients(lines, pooled[...], wqkv_ref[:, : 2 * width], coef_ref)
 
     rows_y = pl.ds(pl.multiple_of(lines[0] + gy * ny, 8), ny)
@@ -311,21 +318,36 @@
     up(0, 0)
     back_in[gx] = back_out[gx]
 
+    def to_cores(src, lane, chunk):
+        for off in range(1, ck):
+            pltpu.make_async_remote_copy(
+                src,
+                gathered.at[lane, chunk],
+                send.at[5],
+                recv.at[5],
+                device_id=(gx, gy, lax.rem(gz + off, ck)),
+                device_id_type=MESH,
+            ).start()
+
     def forward(chunk):
-        def send_chunk(other, carry):
-            to = lax.rem(lane_of + other, group)
+        for off in range(1, cj):
             pltpu.make_async_remote_copy(
                 back_in.at[chunk],
                 gathered.at[lane_of, chunk],
                 send.at[5],
-                recv.at[5],
-                device_id=(gx, to // ck, to % ck),
+                cross_recv.at[gy, chunk],
+                device_id=(gx, lax.rem(gy + off, cj), gz),
                 device_id_type=MESH,
             ).start()
-            return carry
-
-        lax.fori_loop(1, group, send_chunk, 0)
+        to_cores(back_in.at[chunk], lane_of, chunk)
         gathered[lane_of, chunk] = back_in[chunk]
+
+    def relay(chunk):
+        for off in range(1, cj):
+            j = lax.rem(gy + off, cj)
+            lane = j * ck + gz
+            wait_bytes(gathered.at[lane, chunk], cross_recv.at[j, chunk])
+            to_cores(gathered.at[lane, chunk], lane, chunk)
 
     forward(gx)
 
@@ -336,7 +358,14 @@
         return carry
 
     lax.fori_loop(1, ci, arrive, 0)
-    wait_bytes(gathered.at[pl.ds(0, group - 1)], recv.at[5])
+
+    def pass_on(off, carry):
+        relay(lax.rem(gx + ci - off, ci))
+        return carry
+
+    lax.fori_loop(0, ci, pass_on, 0)
+    if ck > 1:
+        wait_bytes(gathered.at[pl.ds(0, cj * (ck - 1))], recv.at[5])
     for g in range(group):
         for q in range(ci):
             at = (g * ci + q) * rows
@@ -375,6 +404,7 @@
     mask = jnp.broadcast_to(jnp.where(head_mask(width, rank), 1.0, 0.0), (HEADS, rank, width)).astype(BF16)
     state = in_ref[0].reshape(rank, rank, width)
     avg = averaging(width)
+    twice_avg = jnp.concatenate([avg, avg], axis=0)
     for y in range(0, ny, 2):
         wide = []
         for e in range(2):
@@ -383,14 +413,14 @@
         pair = dot(query_z[...], jnp.concatenate(wide, axis=1)).astype(BF16)
         mixed[y] = pair[:, :width]
         mixed[y + 1] = pair[:, width:]
-    group = 4
+    group = ny
     for g in range(0, ny, group):
         rows = group * nz
         tok = tok_ref[0, g : g + group].reshape(rows, width).astype(F32)
         resid = tok + dot(mixed[g : g + group].reshape(rows, width), wo_ref[...])
         high = resid.astype(BF16)
         low = (resid - high.astype(F32)).astype(BF16)
-        cent = resid - (dot(high, avg) + dot(low, avg))
+        cent = resid - dot(jnp.concatenate([high, low], axis=1), twice_avg)
         var = dot((cent * cent).astype(BF16), avg)
         inner = (cent * lax.rsqrt(var + EPS)).astype(BF16)
         gate = dot(inner, wgu_ref[:, :ff]).astype(BF16)
@@ -458,6 +488,7 @@
             pltpu.SemaphoreType.DMA((6,)),
             pltpu.SemaphoreType.DMA((6,)),
             pltpu.SemaphoreType.DMA((sizes[0],)),
+            pltpu.SemaphoreType.DMA((sizes[1], sizes[0])),
         ],
         compiler_params=params(collective_id=0, has_side_effects=True),
         name="attend",

time: 74.2 us -> 61.1 us (0.82)
  Pallas kernels: 74 us -> 61 us
    pallas_call x1, Pallas kernels: 27.3 us -> 16.1 us  [body(): pl.pallas_call(functools.partial(finish_kernel, lines), grid=(nx,), in_sp...]
    pallas_call x1, Pallas kernels: 46.7 us -> 44.9 us  [body(): pl.pallas_call(functools.partial(attend_kernel, sizes, lines), in_specs=[...]
where the time goes in v4:
time: 61.1 us; the launch traced here: 61 us
  Pallas kernels  61 us (100%)
    pallas_call x1, Pallas kernels, body(): pl.pallas_call(functools.partial(attend_kernel, sizes, lines), in_specs=[...  44.9 us
    pallas_call x1, Pallas kernels, body(): pl.pallas_call(functools.partial(finish_kernel, lines), grid=(nx,), in_sp...  16.1 us

profile of v4, /device:TPU:0, one launch (start us, length us, event | category | flops | bytes accessed | tf_op | source)
XLA Modules:
  0.0 61.0 jit_solution(2279534123230351792)
XLA Ops:
  0.0 44.9 %attend.1 = (f32[8,256,128]{2,1,0:T(8,128)}, f32[224,256]{1,0:T(8,128)}) custom-call(bf16[8,16,64,128]{3,2,1,0:T(8,128)(2,1)} %tok_ref.3, bf16[128,384]{1,0:T(8,128)(2,1)} %wqkv_ref.1), custom_call_target="tpu_custom_call" | custom-call | tf_op jit(solution)/shard_map/attend/pallas_call | solution.py:456
  44.9 16.1 %finish.1 = bf16[8,16,64,128]{3,2,1,0:T(8,128)(2,1)} custom-call(f32[224,256]{1,0:T(8,128)} %get-tuple-element.7.coef_ref, f32[8,256,128]{2,1,0:T(8,128)} %get-tuple-element.8.in_ref, bf16[8,16,64,128]{3,2,1,0:T(8,128)(2,1)} %tok_ref.3, bf16[128,128]{1,0:T(8,128)(2,1)} %wo_ref.1, bf16[128,1024]{1,0:T(8,128)(2,1)} %wgu_ref.1, bf16[512,128]{1,0:T(8,128)(2,1)} %wd_ref.1), custom_call_target="tpu_custom_call" | custom-call | tf_op jit(solution)/shard_map/finish/pallas_call | solution.py:497

commit v5 on v4

--- a/solution.py
+++ b/solution.py
@@ -29,14 +29,21 @@
     return lane // rank == lax.broadcasted_iota(jnp.int32, shape, 0)
 
 
-def spread_lanes(coef, out_ref, rank):
-    width = coef.shape[-1]
-    row = lax.broadcasted_iota(jnp.int32, (width, width), 0)
-    lane = lax.broadcasted_iota(jnp.int32, (width, width), 1)
-    same = row // rank == lane // rank
-    for d in range(rank):
-        pick = jnp.where(same & (row % rank == d), 1.0, 0.0).astype(BF16)
-        out_ref[d] = dot(coef.astype(BF16), pick)
+def spread_lanes(coefs, out_refs, rank):
+    stacked = jnp.concatenate([c.astype(BF16) for c in coefs], axis=0)
+    width = stacked.shape[-1]
+    row = lax.broadcasted_iota(jnp.int32, (width, 2 * width), 0)
+    lane = lax.broadcasted_iota(jnp.int32, (width, 2 * width), 1)
+    same = row // rank == lane % width // rank
+    index = row % rank - lane // width
+    for d in range(0, rank, 2):
+        wide = dot(stacked, jnp.where(same & (index == d), 1.0, 0.0).astype(BF16))
+        start = 0
+        for coef, out_ref in zip(coefs, out_refs):
+            rows = coef.shape[0]
+            for e in range(2):
+                out_ref[d + e] = wide[start : start + rows, e * width : (e + 1) * width]
+            start += rows
 
 
 def coefficients(lines, pool, w_qk, out_ref):
@@ -124,7 +131,7 @@
     pool_z[...] = jnp.zeros_like(pool_z)
     give[...] = jnp.zeros_like(give)
 
-    piece = 4
+    piece = ny
 
     def normalise(x, carry):
         by_y, by_z = [], jnp.zeros((nz, width), F32)
@@ -227,7 +234,12 @@
 
     rows_y = pl.ds(pl.multiple_of(lines[0] + gy * ny, 8), ny)
     rows_z = pl.ds(pl.multiple_of(lines[0] + lines[1] + gz * nz, 8), nz)
-    spread_lanes(coef_ref[rows_y, width:], key_y, rank)
+    line_x = lines[0]
+    spread_lanes(
+        [coef_ref[:line_x, :width], coef_ref[:line_x, width:], coef_ref[rows_y, width:]],
+        [query_x, key_x, key_y],
+        rank,
+    )
     key_z[...] = coef_ref[rows_z, width:].T.astype(BF16)
     mask = head_mask(width, rank)
     share = rank // group
@@ -260,8 +272,6 @@
         return carry
 
     lax.fori_loop(0, nx, compress, 0)
-    spread_lanes(coef_ref[: lines[0], :width], query_x, rank)
-    spread_lanes(coef_ref[: lines[0], width:], key_x, rank)
     wait_bytes(part_in.at[pl.ds(0, group - 1)], recv.at[2])
 
     rows = share * rank // ci
@@ -389,7 +399,7 @@
 def finish_kernel(
     lines, coef_ref, in_ref, tok_ref, wo_ref, wgu_ref, wd_ref, out_ref, query_y, query_z, mixed
 ):
-    _, ny, nz, width = tok_ref.shape
+    held, ny, nz, width = tok_ref.shape
     rank = width // HEADS
     ff = wd_ref.shape[0]
 
@@ -398,43 +408,42 @@
         gy, gz = lax.axis_index("gy"), lax.axis_index("gz")
         rows_y = pl.ds(pl.multiple_of(lines[0] + gy * ny, 8), ny)
         rows_z = pl.ds(pl.multiple_of(lines[0] + lines[1] + gz * nz, 8), nz)
-        spread_lanes(coef_ref[rows_y, :width], query_y, rank)
+        spread_lanes([coef_ref[rows_y, :width]], [query_y], rank)
         query_z[...] = coef_ref[rows_z, :width].astype(BF16)
 
     mask = jnp.broadcast_to(jnp.where(head_mask(width, rank), 1.0, 0.0), (HEADS, rank, width)).astype(BF16)
-    state = in_ref[0].reshape(rank, rank, width)
     avg = averaging(width)
     twice_avg = jnp.concatenate([avg, avg], axis=0)
-    for y in range(0, ny, 2):
-        wide = []
-        for e in range(2):
-            line = jnp.sum(query_y[:, y + e : y + e + 1, :] * state, axis=0).astype(BF16)
-            wide.append((mask * line[None]).reshape(HEADS * rank, width))
-        pair = dot(query_z[...], jnp.concatenate(wide, axis=1)).astype(BF16)
-        mixed[y] = pair[:, :width]
-        mixed[y + 1] = pair[:, width:]
-    group = ny
-    for g in range(0, ny, group):
-        rows = group * nz
-        tok = tok_ref[0, g : g + group].reshape(rows, width).astype(F32)
-        resid = tok + dot(mixed[g : g + group].reshape(rows, width), wo_ref[...])
-        high = resid.astype(BF16)
-        low = (resid - high.astype(F32)).astype(BF16)
-        cent = resid - dot(jnp.concatenate([high, low], axis=1), twice_avg)
-        var = dot((cent * cent).astype(BF16), avg)
-        inner = (cent * lax.rsqrt(var + EPS)).astype(BF16)
-        gate = dot(inner, wgu_ref[:, :ff]).astype(BF16)
-        up = dot(inner, wgu_ref[:, ff:]).astype(BF16)
-        result = resid + 0.5 * dot(twice_gelu_times(gate, up), wd_ref[...])
-        out_ref[0, g : g + group] = result.astype(BF16).reshape(group, nz, width)
+    for x in range(held):
+        state = in_ref[x].reshape(rank, rank, width)
+        for y in range(0, ny, 2):
+            wide = []
+            for e in range(2):
+                line = jnp.sum(query_y[:, y + e : y + e + 1, :] * state, axis=0).astype(BF16)
+                wide.append((mask * line[None]).reshape(HEADS * rank, width))
+            pair = dot(query_z[...], jnp.concatenate(wide, axis=1)).astype(BF16)
+            mixed[x, y] = pair[:, :width]
+            mixed[x, y + 1] = pair[:, width:]
+    rows = held * ny * nz
+    tok = tok_ref[...].reshape(rows, width).astype(F32)
+    resid = tok + dot(mixed[...].reshape(rows, width), wo_ref[...])
+    high = resid.astype(BF16)
+    low = (resid - high.astype(F32)).astype(BF16)
+    cent = resid - dot(jnp.concatenate([high, low], axis=1), twice_avg)
+    var = dot((cent * cent).astype(BF16), avg)
+    inner = (cent * lax.rsqrt(var + EPS)).astype(BF16)
+    gate = dot(inner, wgu_ref[:, :ff]).astype(BF16)
+    up = dot(inner, wgu_ref[:, ff:]).astype(BF16)
+    result = resid + 0.5 * dot(twice_gelu_times(gate, up), wd_ref[...])
+    out_ref[...] = result.astype(BF16).reshape(out_ref.shape)
 
 
 def whole(shape):
     return pl.BlockSpec(shape, lambda i: (0,) * len(shape))
 
 
-def slab(shape):
-    return pl.BlockSpec((1,) + shape[1:], lambda i: (i,) + (0,) * (len(shape) - 1))
+def slab(shape, held):
+    return pl.BlockSpec((held,) + shape[1:], lambda i: (i,) + (0,) * (len(shape) - 1))
 
 
 def params(**more):
@@ -494,23 +503,24 @@
         name="attend",
     )(tokens, w_qkv)
 
+    held = 2 if nx % 2 == 0 else 1
     return pl.pallas_call(
         functools.partial(finish_kernel, lines),
-        grid=(nx,),
+        grid=(nx // held,),
         in_specs=[
             whole(coef.shape),
-            slab(small),
-            slab(tokens.shape),
+            slab(small, held),
+            slab(tokens.shape, held),
             whole(w_out.shape),
             whole(w_gate_up.shape),
             whole(w_down.shape),
         ],
-        out_specs=slab(tokens.shape),
+        out_specs=slab(tokens.shape, held),
         out_shape=jax.ShapeDtypeStruct(tokens.shape, BF16),
         scratch_shapes=[
             pltpu.VMEM((rank, ny, width), F32),
             pltpu.VMEM((nz, width), BF16),
-            pltpu.VMEM((ny, nz, width), BF16),
+            pltpu.VMEM((held, ny, nz, width), BF16),
         ],
         compiler_params=params(),
         name="finish",

time: 61.1 us -> 59.1 us (0.967)
  Pallas kernels: 61 us -> 58.9 us
    pallas_call x1, Pallas kernels: 16.1 us -> 14.1 us  [body(): pl.pallas_call(functools.partial(finish_kernel, lines), grid=(nx // held,...]
where the time goes in v5:
time: 59.1 us; the launch traced here: 58.9 us
  Pallas kernels  58.9 us (100%)
    pallas_call x1, Pallas kernels, body(): pl.pallas_call(functools.partial(attend_kernel, sizes, lines), in_specs=[...  44.8 us
    pallas_call x1, Pallas kernels, body(): pl.pallas_call(functools.partial(finish_kernel, lines), grid=(nx // held,...  14.1 us

profile of v5, /device:TPU:0, one launch (start us, length us, event | category | flops | bytes accessed | tf_op | source)
XLA Modules:
  0.0 58.9 jit_solution(7148526534606031854)
XLA Ops:
  0.0 44.8 %attend.1 = (f32[8,256,128]{2,1,0:T(8,128)}, f32[224,256]{1,0:T(8,128)}) custom-call(bf16[8,16,64,128]{3,2,1,0:T(8,128)(2,1)} %tok_ref.3, bf16[128,384]{1,0:T(8,128)(2,1)} %wqkv_ref.1), custom_call_target="tpu_custom_call" | custom-call | tf_op jit(solution)/shard_map/attend/pallas_call | solution.py:465
  44.8 14.1 %finish.1 = bf16[8,16,64,128]{3,2,1,0:T(8,128)(2,1)} custom-call(f32[224,256]{1,0:T(8,128)} %get-tuple-element.7.coef_ref, f32[8,256,128]{2,1,0:T(8,128)} %get-tuple-element.8.in_ref, bf16[8,16,64,128]{3,2,1,0:T(8,128)(2,1)} %tok_ref.3, bf16[128,128]{1,0:T(8,128)(2,1)} %wo_ref.1, bf16[128,1024]{1,0:T(8,128)(2,1)} %wgu_ref.1, bf16[512,128]{1,0:T(8,128)(2,1)} %wd_ref.1), custom_call_target="tpu_custom_call" | custom-call | tf_op jit(solution)/shard_map/finish/pallas_call | solution.py:507

commit v6 on v5

--- a/solution.py
+++ b/solution.py
@@ -77,9 +77,8 @@
     out_ref,
     coef_ref,
     value,
-    pool_x,
-    pool_y,
-    pool_z,
+    local,
+    near,
     give,
     take,
     owned,
@@ -105,30 +104,28 @@
     cross_recv,
 ):
     ci, cj, ck = sizes
-    count = ci * cj * ck
     group = cj * ck
     nx, ny, nz, width = tok_ref.shape
+    padded = give.shape[1]
     rank = width // HEADS
     gx, gy, gz = (lax.axis_index(a) for a in ("gx", "gy", "gz"))
-    me = (gx * cj + gy) * ck + gz
     lane_of = gy * ck + gz
 
-    def place(flat):
-        return lax.div(flat, group), lax.rem(lax.div(flat, ck), cj), lax.rem(flat, ck)
+    def in_group(off):
+        lane = lax.rem(lane_of + off, group)
+        return (gx, lax.div(lane, ck), lax.rem(lane, ck))
+
+    def along_x(off):
+        return (lax.rem(gx + off, ci), gy, gz)
 
     barrier = pltpu.get_barrier_semaphore()
-
-    def greet(off, carry):
-        pl.semaphore_signal(
-            barrier, inc=1, device_id=place(lax.rem(me + off, count)), device_id_type=MESH
-        )
-        return carry
-
-    lax.fori_loop(1, count, greet, 0)
+    for off in range(1, group):
+        pl.semaphore_signal(barrier, inc=1, device_id=in_group(off), device_id_type=MESH)
+    for off in range(1, ci):
+        pl.semaphore_signal(barrier, inc=1, device_id=along_x(off), device_id_type=MESH)
 
     avg = averaging(width)
-    pool_y[...] = jnp.zeros_like(pool_y)
-    pool_z[...] = jnp.zeros_like(pool_z)
+    local[...] = jnp.zeros_like(local)
     give[...] = jnp.zeros_like(give)
 
     piece = ny
@@ -145,45 +142,19 @@
             by_y.append(jnp.sum(full, axis=1))
             by_z = by_z + jnp.sum(full, axis=0)
         by_y = jnp.concatenate(by_y, axis=0)
-        pool_x[pl.ds(x, 1), :] = jnp.sum(by_y, axis=0, keepdims=True)
-        pool_y[...] += by_y
-        pool_z[...] += by_z
+        local[pl.ds(x, 1), :] = jnp.sum(by_y, axis=0, keepdims=True)
+        local[nx : nx + ny, :] += by_y
+        local[nx + ny :, :] += by_z
         return carry
 
     lax.fori_loop(0, nx, normalise, 0)
 
-    held_x, held_y, held_z = -(-nx // group), -(-ny // (ci * ck)), -(-nz // (ci * cj))
-
-    def starts(i, j, k):
-        return (
-            jnp.minimum((j * ck + k) * held_x, nx - held_x),
-            jnp.minimum((i * ck + k) * held_y, ny - held_y),
-            jnp.minimum((i * cj + j) * held_z, nz - held_z),
-        )
-
-    def fill(s, carry):
-        at_x, at_y, at_z = starts(*place(s))
-        for r in range(held_x):
-            give[s, r : r + 1, :] = pool_x[pl.ds(at_x + r, 1), :]
-        for r in range(held_y):
-            give[s, held_x + r : held_x + r + 1, :] = pool_y[pl.ds(at_y + r, 1), :]
-        for r in range(held_z):
-            row = held_x + held_y + r
-            give[s, row : row + 1, :] = pool_z[pl.ds(at_z + r, 1), :]
-        return carry
-
-    lax.fori_loop(0, count, fill, 0, unroll=4)
-    pl.semaphore_wait(barrier, count - 1)
-
-    def send_rows(off, carry):
-        to = lax.rem(me + off, count)
+    pl.semaphore_wait(barrier, group - 1 + ci - 1)
+    for off in range(1, group):
         pltpu.make_async_remote_copy(
-            give.at[to], take.at[me], send.at[0], recv.at[0], device_id=place(to), device_id_type=MESH
+            local, near.at[lane_of], send.at[0], recv.at[0], device_id=in_group(off), device_id_type=MESH
         ).start()
-        return carry
-
-    lax.fori_loop(1, count, send_rows, 0, unroll=4)
-    take[me] = give[me]
+    near[lane_of] = local[...]
 
     def project(x, carry):
         normed = value[x].reshape(ny * nz, width)
@@ -191,45 +162,40 @@
         return carry
 
     lax.fori_loop(0, nx, project, 0)
-    wait_bytes(take.at[pl.ds(0, count - 1)], recv.at[0])
-
-    row = lax.broadcasted_iota(jnp.int32, owned.shape, 0)
-
-    def add_rows(s, acc):
-        i, j, k = place(s)
-        ours = jnp.where(
-            row < held_x,
-            (i == gx).astype(jnp.int32),
-            jnp.where(row < held_x + held_y, (j == gy).astype(jnp.int32), (k == gz).astype(jnp.int32)),
-        )
-        return acc + jnp.where(ours > 0, take[s], 0.0)
-
-    owned[...] = lax.fori_loop(0, count, add_rows, jnp.zeros(owned.shape, F32), unroll=4)
-
-    def send_owned(off, carry):
-        to = lax.rem(me + off, count)
+    wait_bytes(near.at[pl.ds(0, group - 1)], recv.at[0])
+
+    def over(lanes, start, stop):
+        return functools.reduce(lambda u, v: u + v, [near[g, start:stop, :] for g in lanes])
+
+    sum_y = [over([j * ck + k for k in range(ck)], nx, nx + ny) for j in range(cj)]
+    sum_z = [over([j * ck + k for j in range(cj)], nx + ny, nx + ny + nz) for k in range(ck)]
+    pooled[lines[0] : lines[0] + lines[1], :] = jnp.concatenate(sum_y, axis=0)
+    pooled[lines[0] + lines[1] :, :] = jnp.concatenate(sum_z, axis=0)
+
+    part_y, part_z = lines[1] // ci, lines[2] // ci
+    base_y, base_z = lines[0], lines[0] + lines[1]
+    for q in range(ci):
+        give[q, :part_y, :] = pooled[base_y + q * part_y : base_y + (q + 1) * part_y, :]
+        give[q, part_y : part_y + part_z, :] = pooled[base_z + q * part_z : base_z + (q + 1) * part_z, :]
+    for off in range(1, ci):
+        to = along_x(off)
         pltpu.make_async_remote_copy(
-            owned, spread.at[me], send.at[1], recv.at[1], device_id=place(to), device_id_type=MESH
+            give.at[to[0]], take.at[gx], send.at[1], recv.at[1], device_id=to, device_id_type=MESH
         ).start()
-        return carry
-
-    lax.fori_loop(1, count, send_owned, 0, unroll=4)
-    spread[me] = owned[...]
-    wait_bytes(spread.at[pl.ds(0, count - 1)], recv.at[1])
-
-    def unfold(s, carry):
-        i, j, k = place(s)
-        at_x, at_y, at_z = starts(i, j, k)
-        for r in range(held_x):
-            pooled[pl.ds(i * nx + at_x + r, 1), :] = spread[s, r : r + 1, :]
-        for r in range(held_y):
-            pooled[pl.ds(lines[0] + j * ny + at_y + r, 1), :] = spread[s, held_x + r : held_x + r + 1, :]
-        for r in range(held_z):
-            row = held_x + held_y + r
-            pooled[pl.ds(lines[0] + lines[1] + k * nz + at_z + r, 1), :] = spread[s, row : row + 1, :]
-        return carry
-
-    lax.fori_loop(0, count, unfold, 0, unroll=4)
+    take[gx] = give[gx]
+    owned[padded:, :] = over(range(group), 0, nx)
+    wait_bytes(take.at[pl.ds(0, ci - 1)], recv.at[1])
+    owned[:padded, :] = jnp.sum(take[...], axis=0)
+    for off in range(1, ci):
+        pltpu.make_async_remote_copy(
+            owned, spread.at[gx], send.at[6], recv.at[6], device_id=along_x(off), device_id_type=MESH
+        ).start()
+    spread[gx] = owned[...]
+    wait_bytes(spread.at[pl.ds(0, ci - 1)], recv.at[6])
+    for q in range(ci):
+        pooled[q * nx : (q + 1) * nx, :] = spread[q, padded:, :]
+        pooled[base_y + q * part_y : base_y + (q + 1) * part_y, :] = spread[q, :part_y, :]
+        pooled[base_z + q * part_z : base_z + (q + 1) * part_z, :] = spread[q, part_y : part_y + part_z, :]
     coefficients(lines, pooled[...], wqkv_ref[:, : 2 * width], coef_ref)
 
     rows_y = pl.ds(pl.multiple_of(lines[0] + gy * ny, 8), ny)
@@ -381,8 +347,9 @@
             at = (g * ci + q) * rows
             out_ref[:, at : at + rows, :] = gathered[g, q].astype(F32).reshape(nx, rows, width)
 
-    wait_bytes(give.at[pl.ds(0, count - 1)], send.at[0])
-    wait_bytes(spread.at[pl.ds(0, count - 1)], send.at[1])
+    wait_bytes(near.at[pl.ds(0, group - 1)], send.at[0])
+    wait_bytes(take.at[pl.ds(0, ci - 1)], send.at[1])
+    wait_bytes(spread.at[pl.ds(0, ci - 1)], send.at[6])
     wait_bytes(part_in.at[pl.ds(0, group - 1)], send.at[2])
     wait_bytes(x_out.at[pl.ds(0, ci - 1)], send.at[3])
     wait_bytes(back_out.at[pl.ds(0, ci - 1)], send.at[4])
@@ -456,9 +423,8 @@
     lines = (nx * lax.axis_size("gx"), ny * lax.axis_size("gy"), nz * lax.axis_size("gz"))
     total = sum(lines)
     sizes = tuple(lax.axis_size(a) for a in ("gx", "gy", "gz"))
-    count, group = math.prod(sizes), sizes[1] * sizes[2]
-    held = -(-nx // group) - (-ny // (sizes[0] * sizes[2])) - (-nz // (sizes[0] * sizes[1]))
-    held = -(-held // 8) * 8
+    group = sizes[1] * sizes[2]
+    padded = -(-(lines[1] // sizes[0] + lines[2] // sizes[0]) // 8) * 8
     share = rank // group
     rows = share * rank // sizes[0]
     small = (nx, rank * rank, width)
@@ -472,13 +438,12 @@
         ],
         scratch_shapes=[
             pltpu.VMEM(tokens.shape, BF16),
-            pltpu.VMEM((nx, width), F32),
-            pltpu.VMEM((ny, width), F32),
-            pltpu.VMEM((nz, width), F32),
-            pltpu.VMEM((count, held, width), F32),
-            pltpu.VMEM((count, held, width), F32),
-            pltpu.VMEM((held, width), F32),
-            pltpu.VMEM((count, held, width), F32),
+            pltpu.VMEM((nx + ny + nz, width), F32),
+            pltpu.VMEM((group, nx + ny + nz, width), F32),
+            pltpu.VMEM((sizes[0], padded, width), F32),
+            pltpu.VMEM((sizes[0], padded, width), F32),
+            pltpu.VMEM((padded + nx, width), F32),
+            pltpu.VMEM((sizes[0], padded + nx, width), F32),
             pltpu.VMEM((total, width), F32),
             pltpu.VMEM((rank, ny, width), F32),
             pltpu.VMEM((width, nz), BF16),
@@ -494,8 +459,8 @@
             pltpu.VMEM((sizes[0], nx * rows, width), BF16),
             pltpu.VMEM((sizes[0], nx * rows, width), BF16),
             pltpu.VMEM((group, sizes[0], nx * rows, width), BF16),
-            pltpu.SemaphoreType.DMA((6,)),
-            pltpu.SemaphoreType.DMA((6,)),
+            pltpu.SemaphoreType.DMA((7,)),
+            pltpu.SemaphoreType.DMA((7,)),
             pltpu.SemaphoreType.DMA((sizes[0],)),
             pltpu.SemaphoreType.DMA((sizes[1], sizes[0])),
         ],

time: 59.1 us -> 59.3 us (level)
  no operation moved by 1% of the time
where the time goes in v6:
time: 59.3 us; the launch traced here: 59.2 us
  Pallas kernels  59.1 us (100%)
    pallas_call x1, Pallas kernels, body(): pl.pallas_call(functools.partial(attend_kernel, sizes, lines), in_specs=[...  45.1 us
    pallas_call x1, Pallas kernels, body(): pl.pallas_call(functools.partial(finish_kernel, lines), grid=(nx // held,...  14.1 us

profile of v6, /device:TPU:0, one launch (start us, length us, event | category | flops | bytes accessed | tf_op | source)
XLA Modules:
  0.0 59.2 jit_solution(10532111685055151822)
XLA Ops:
  0.0 45.1 %attend.1 = (f32[8,256,128]{2,1,0:T(8,128)}, f32[224,256]{1,0:T(8,128)}) custom-call(bf16[8,16,64,128]{3,2,1,0:T(8,128)(2,1)} %tok_ref.3, bf16[128,384]{1,0:T(8,128)(2,1)} %wqkv_ref.1), custom_call_target="tpu_custom_call" | custom-call | tf_op jit(solution)/shard_map/attend/pallas_call | solution.py:431
  45.1 14.1 %finish.1 = bf16[8,16,64,128]{3,2,1,0:T(8,128)(2,1)} custom-call(f32[224,256]{1,0:T(8,128)} %get-tuple-element.7.coef_ref, f32[8,256,128]{2,1,0:T(8,128)} %get-tuple-element.8.in_ref, bf16[8,16,64,128]{3,2,1,0:T(8,128)(2,1)} %tok_ref.3, bf16[128,128]{1,0:T(8,128)(2,1)} %wo_ref.1, bf16[128,1024]{1,0:T(8,128)(2,1)} %wgu_ref.1, bf16[512,128]{1,0:T(8,128)(2,1)} %wd_ref.1), custom_call_target="tpu_custom_call" | custom-call | tf_op jit(solution)/shard_map/finish/pallas_call | solution.py:472

commit v7 on v6

--- a/solution.py
+++ b/solution.py
@@ -216,10 +216,12 @@
             for e in range(2):
                 full = pair[:, e * width : (e + 1) * width].reshape(HEADS, rank, width)
                 state[y + e] = jnp.sum(jnp.where(mask, full, 0.0), axis=0)
-        acc = jnp.zeros((rank, rank, width), F32)
-        for y in range(ny):
-            acc = acc + key_y[:, y : y + 1, :] * state[y][None, :, :]
-        part_out[x] = acc.astype(BF16)
+        half = rank // 2
+        for d in range(0, rank, half):
+            acc = jnp.zeros((half, rank, width), F32)
+            for y in range(ny):
+                acc = acc + key_y[d : d + half, y : y + 1, :] * state[y][None, :, :]
+            part_out[x, d : d + half] = acc.astype(BF16)
 
         def send_share(off, carry):
             to = lax.rem(lane_of + off, group)
@@ -468,7 +470,7 @@
         name="attend",
     )(tokens, w_qkv)
 
-    held = 2 if nx % 2 == 0 else 1
+    held = math.gcd(nx, 4)
     return pl.pallas_call(
         functools.partial(finish_kernel, lines),
         grid=(nx // held,),

time: 59.3 us -> 59.2 us (level)
  no operation moved by 1% of the time
where the time goes in v7:
time: 59.2 us; the launch traced here: 59 us
  Pallas kernels  59 us (100%)
    pallas_call x1, Pallas kernels, body(): pl.pallas_call(functools.partial(attend_kernel, sizes, lines), in_specs=[...  45 us
    pallas_call x1, Pallas kernels, body(): pl.pallas_call(functools.partial(finish_kernel, lines), grid=(nx // held,...  14 us

profile of v7, /device:TPU:0, one launch (start us, length us, event | category | flops | bytes accessed | tf_op | source)
XLA Modules:
  0.0 59.0 jit_solution(7512674194063029617)
XLA Ops:
  0.0 45.0 %attend.1 = (f32[8,256,128]{2,1,0:T(8,128)}, f32[224,256]{1,0:T(8,128)}) custom-call(bf16[8,16,64,128]{3,2,1,0:T(8,128)(2,1)} %tok_ref.3, bf16[128,384]{1,0:T(8,128)(2,1)} %wqkv_ref.1), custom_call_target="tpu_custom_call" | custom-call | tf_op jit(solution)/shard_map/attend/pallas_call | solution.py:433
  45.0 14.0 %finish.1 = bf16[8,16,64,128]{3,2,1,0:T(8,128)(2,1)} custom-call(f32[224,256]{1,0:T(8,128)} %get-tuple-element.7.coef_ref, f32[8,256,128]{2,1,0:T(8,128)} %get-tuple-element.8.in_ref, bf16[8,16,64,128]{3,2,1,0:T(8,128)(2,1)} %tok_ref.3, bf16[128,128]{1,0:T(8,128)(2,1)} %wo_ref.1, bf16[128,1024]{1,0:T(8,128)(2,1)} %wgu_ref.1, bf16[512,128]{1,0:T(8,128)(2,1)} %wd_ref.1), custom_call_target="tpu_custom_call" | custom-call | tf_op jit(solution)/shard_map/finish/pallas_call | solution.py:474
